TPU v7x, 32 devices: a whole 2x2x4 slice. The times are simulated.
32 devices in a mesh: tm: 16 (over z, y, core), space: 2 (over x).
Axes of the slice: x: 2, y: 2, z: 4, core: 2. Of those that a mesh axis runs over, the one named last changes fastest.
Arguments:
- start_state: float32 [16, 64, 2048], P('tm', None, 'space'), may hold values from -1.2 to 1.2
- stiffness: float32 [64, 64], replicated, may hold values from -0.75 to 0.75
- lifting: float32 [64, 96], replicated, may hold values from -0.625 to 0.625
- coarse: float32 [64, 64], replicated
- neighbor: int32 [6, 2048], P(None, 'space'), may hold values from 0 to 2047, as said below
- orientation: int32 [6, 2048], P(None, 'space'), may hold values from 0 to 7
- send_low: int32 [1024], P('space'), may hold values from 0 to 1023, as said below
- send_high: int32 [1024], P('space'), may hold values from 0 to 1023, as said below
Outputs:
- end_state: float32 [16, 64, 2048], P('tm', None, 'space')
Inputs may be any that keep to these rules, and one draw needn't show every extreme that they name: `send_low`: distinct local slots of one partition, 512 per partition; the lower boundary elements of a partition are the upper neighbours, across face 1, of the upper boundary elements of the partition below, in the same order. `send_high`: distinct local slots of one partition, 512 per partition. `neighbor`: values of 1024 or more occur only for face 0 (first 512 halo slots) and face 1 (next 512 halo slots); each halo slot is named by exactly one element.
All inputs are finite; a program needn't handle non-finite values.
Results may differ from a plain program's by a relative error of at most 0.00015.
Values sent between devices are 32-bit elements; how exact they have to be, the bound alone decides.
A program may use at most 64 MiB of HBM per device.

v0:
```python
import jax
import jax.numpy as jnp
from jax import lax
from jax.sharding import PartitionSpec as P

STEPS = 3


time_step = 0.05


def with_halo(shard, sides, width):
    for axis, dim in sides:
        peers, length = (lax.axis_size(axis), shard.shape[dim])
        up = [(i, (i + 1) % peers) for i in range(peers)]
        down = [(j, i) for i, j in up]
        last = lax.slice_in_dim(shard, length - width, length, axis=dim)
        initial = lax.slice_in_dim(shard, 0, width, axis=dim)
        before = lax.ppermute(last, axis, up)
        after = lax.ppermute(initial, axis, down)
        shard = jnp.concatenate([before, shard, after], axis=dim)
    return shard


def from_behind(shard, axis, by):
    peers = lax.axis_size(axis)
    pairs = [(i, i + by) for i in range(peers) if 0 <= i + by < peers]
    return lax.ppermute(shard, axis, pairs)


def product(matrix, vector):
    return jnp.dot(
        matrix, vector, precision=lax.Precision.HIGHEST, preferred_element_type=jnp.float32
    )


def face_traces(state_now):
    elements = state_now.shape[1]
    cube_view = state_now.reshape(4, 4, 4, elements)
    return [
        cube_view[0],
        cube_view[3],
        cube_view[:, 0],
        cube_view[:, 3],
        cube_view[:, :, 0],
        cube_view[:, :, 3],
    ]


def oriented_all(traces, codes):
    summed = jnp.zeros_like(traces)
    for variant in range(8):
        turned = traces
        if variant & 4:
            turned = jnp.swapaxes(turned, 1, 2)
        if variant & 1:
            turned = turned[:, ::-1]
        if variant & 2:
            turned = turned[:, :, ::-1]
        summed = summed + jnp.where(codes[:, None, None, :] == variant, turned, 0.0)
    return summed


def fine_step(state_now, stiffness, lifting, neighbor, orientation, send_low, send_high):
    elements = state_now.shape[1]
    own_list = face_traces(state_now)
    own_stack = jnp.stack(own_list)
    flat_stack = own_stack.reshape(6, 16, elements)
    outgoing = jnp.stack(
        [jnp.take(flat_stack[0], send_low, axis=1), jnp.take(flat_stack[1], send_high, axis=1)]
    )
    received = with_halo(outgoing, (("space", 0),), 1)
    opposite = flat_stack[jnp.array([1, 0, 3, 2, 5, 4])]
    halo_part = jnp.concatenate([received[0], received[3]], axis=1)
    bound = halo_part.shape[1]
    extended = jnp.concatenate(
        [opposite, jnp.broadcast_to(halo_part[None], (6, 16, bound))], axis=2
    )
    beside = jnp.take_along_axis(extended, neighbor[:, None, :], axis=2).reshape(6, 4, 4, elements)
    jumps = oriented_all(beside, orientation) - own_stack
    stacked = jumps.reshape(96, elements)
    rate = (
        product(stiffness, state_now)
        + product(lifting, stacked)
        + state_now
        - state_now * state_now * state_now
    )
    return state_now + time_step * rate


def shards(start_state, stiffness, lifting, coarse, neighbor, orientation, send_low, send_high):
    state_start = start_state[0]
    fine_state = state_start
    for step_id in range(STEPS):
        fine_state = fine_step(
            fine_state, stiffness, lifting, neighbor, orientation, send_low, send_high
        )
    defect = fine_state - product(coarse, state_start)
    is_first = lax.axis_index("tm") == 0

    def turn(turn_id, current):
        advanced = product(coarse, current) + defect
        arrived = from_behind(advanced, "tm", 1)
        return jnp.where(is_first, state_start, arrived)

    current = lax.fori_loop(0, lax.axis_size("tm") - 1, turn, state_start)
    end_now = product(coarse, current) + defect
    return end_now[None]


def solution(mesh):
    return jax.shard_map(
        shards,
        mesh=mesh,
        in_specs=(
            P("tm", None, "space"),
            P(),
            P(),
            P(),
            P(None, "space"),
            P(None, "space"),
            P("space"),
            P("space"),
        ),
        out_specs=P("tm", None, "space"),
        check_vma=False,
    )
```

profile of v0, /device:TPU:25, one launch (start us, length us, event | category | flops | bytes accessed | tf_op | source)
XLA Modules:
  0.0 489.3 jit_solution(5678332601789200304)
XLA Ops:
  1.4 0.8 constant_dynamic-update-slice_fusion.3
  2.3 0.9 constant_dynamic-update-slice_fusion.2
  4.1 1.0 gather_fusion.3
  5.3 1.3 collective-permute-start.1
  7.4 1.0 gather_fusion.4
  11.6 1.0 collective-permute-done.1
  12.6 5.6 %collective-permute-done.2 = f32[1,16,512]{1,2,0:T(8,128)} collective-permute-done((f32[1,16,512]{1,2,0:T(8,128)S(1)}, f32[1,16,512]{1,2,0:T(8,128)}, u32[]{:S(2)}, u32[]{:S(2)}) %collective-permute-start.2) | collective-permute-done | bytes 32800 | tf_op jit(solution)/shard_map/ppermute | solution.py:20
  18.2 1.0 copy.88
  19.4 4.0 copy.89
  23.4 89.5 %gather_fusion.5 = f32[6144,16]{1,0:T(8,128)} fusion(f32[6,16,2048]{1,2,0:T(8,128)} %copy.89, s32[6144]{0:T(1024)S(1)} %reshape.255), kind=kCustom, calls=%fused_computation.1.clone | custom fusion | bytes 835584 | tf_op jit(solution)/shard_map/jit(take_along_axis)/gather | solution.py:79
  112.9 4.7 select_bitcast_fusion.2
  117.5 2.7 copy.90
  123.5 1.0 gather_fusion.7
  124.7 1.3 collective-permute-start.4
  126.2 1.0 gather_fusion.6
  128.6 0.9 copy.106
  129.5 0.9 copy.107
  131.1 1.0 copy.100
  132.1 4.5 collective-permute-done.3
  136.8 4.0 copy.101
  140.8 89.5 %gather_fusion.8 = f32[6144,16]{1,0:T(8,128)} fusion(f32[6,16,2048]{1,2,0:T(8,128)} %copy.101, s32[6144]{0:T(1024)S(1)} %reshape.255), kind=kCustom, calls=%fused_computation.7.clone | custom fusion | bytes 835584 | tf_op jit(solution)/shard_map/jit(take_along_axis)/gather | solution.py:79
  230.3 4.7 select_bitcast_fusion.1
  234.9 2.9 copy.102
  240.4 1.0 gather_fusion.9
  241.6 1.3 collective-permute-start.5
  243.1 1.0 gather_fusion.10
  247.0 1.0 copy.111
  248.0 4.7 collective-permute-done.6
  252.9 4.0 copy.113
  256.9 89.5 %gather_fusion.11 = f32[6144,16]{1,0:T(8,128)} fusion(f32[6,16,2048]{1,2,0:T(8,128)} %copy.113, s32[6144]{0:T(1024)S(1)} %reshape.255), kind=kCustom, calls=%fused_computation.8.clone | custom fusion | bytes 835584 | tf_op jit(solution)/shard_map/jit(take_along_axis)/gather | solution.py:79
  346.4 4.7 select_bitcast_fusion
  351.1 2.7 copy.114
  355.4 132.8 %while.10 = (s32[]{:T(128)}, f32[64,1024]{1,0:T(8,128)S(1)}, pred[]{:T(512)}, f32[64,64]{1,0:T(8,128)S(1)}, f32[64,1024]{1,0:T(8,128)S(1)}, /*index=5*/f32[64,1024]{1,0:T(8,128)S(1)}, s32[]{:T(128)}) while((s32[]{:T(128)}, f32[64,1024]{1,0:T(8,128)S(1)}, pred[]{:T(512)}, f32[64,64]{1,0:T(8,128)S(1)}, f32[64,1024]{1,0:T(8,128)S(1)}, ...), condition=%wide.region_1.0_spmd, body=%wide.region_0.3_spmd.sunk | while | flops 50462720 | bytes 2637942 | solution.py:106
  355.8 6.3 %collective-permute-start = (f32[64,1024]{1,0:T(8,128)S(1)}, f32[64,1024]{1,0:T(8,128)S(1)}, u32[]{:S(2)}, u32[]{:S(2)}) collective-permute-start(f32[64,1024]{1,0:T(8,128)S(1)} %convolution_add_fusion.4), channel_id=1, source_target_pairs={{0,2},{2,4},{4,6},{6,8},{8,10},{10,12},{12,14},{14,16},{16,18},{18... | collective-permute-start | bytes 786440 | tf_op jit(solution)/shard_map/while/body/eval_jaxpr/ppermute | solution.py:28
  362.1 3.3 collective-permute-done
  365.8 4.4 collective-permute-start
  370.2 3.3 collective-permute-done
  373.9 4.4 collective-permute-start
  378.4 3.3 collective-permute-done
  382.1 4.4 collective-permute-start
  386.5 3.3 collective-permute-done
  390.2 4.4 collective-permute-start
  394.6 3.5 collective-permute-done
  398.5 4.2 collective-permute-start
  402.7 4.3 collective-permute-done
  407.5 3.3 collective-permute-start
  410.8 5.2 %collective-permute-done = f32[64,1024]{1,0:T(8,128)S(1)} collective-permute-done((f32[64,1024]{1,0:T(8,128)S(1)}, f32[64,1024]{1,0:T(8,128)S(1)}, u32[]{:S(2)}, u32[]{:S(2)}) %collective-permute-start) | collective-permute-done | bytes 262176 | tf_op jit(solution)/shard_map/while/body/eval_jaxpr/ppermute | solution.py:28
  416.5 2.4 collective-permute-start
  418.9 6.1 %collective-permute-done = f32[64,1024]{1,0:T(8,128)S(1)} collective-permute-done((f32[64,1024]{1,0:T(8,128)S(1)}, f32[64,1024]{1,0:T(8,128)S(1)}, u32[]{:S(2)}, u32[]{:S(2)}) %collective-permute-start) | collective-permute-done | bytes 262176 | tf_op jit(solution)/shard_map/while/body/eval_jaxpr/ppermute | solution.py:28
  425.5 1.9 collective-permute-start
  427.4 6.7 %collective-permute-done = f32[64,1024]{1,0:T(8,128)S(1)} collective-permute-done((f32[64,1024]{1,0:T(8,128)S(1)}, f32[64,1024]{1,0:T(8,128)S(1)}, u32[]{:S(2)}, u32[]{:S(2)}) %collective-permute-start) | collective-permute-done | bytes 262176 | tf_op jit(solution)/shard_map/while/body/eval_jaxpr/ppermute | solution.py:28
  434.5 1.9 collective-permute-start
  436.4 6.7 %collective-permute-done = f32[64,1024]{1,0:T(8,128)S(1)} collective-permute-done((f32[64,1024]{1,0:T(8,128)S(1)}, f32[64,1024]{1,0:T(8,128)S(1)}, u32[]{:S(2)}, u32[]{:S(2)}) %collective-permute-start) | collective-permute-done | bytes 262176 | tf_op jit(solution)/shard_map/while/body/eval_jaxpr/ppermute | solution.py:28
  443.5 1.9 collective-permute-start
  445.5 6.7 %collective-permute-done = f32[64,1024]{1,0:T(8,128)S(1)} collective-permute-done((f32[64,1024]{1,0:T(8,128)S(1)}, f32[64,1024]{1,0:T(8,128)S(1)}, u32[]{:S(2)}, u32[]{:S(2)}) %collective-permute-start) | collective-permute-done | bytes 262176 | tf_op jit(solution)/shard_map/while/body/eval_jaxpr/ppermute | solution.py:28
  452.5 1.9 collective-permute-start
  454.5 6.7 %collective-permute-done = f32[64,1024]{1,0:T(8,128)S(1)} collective-permute-done((f32[64,1024]{1,0:T(8,128)S(1)}, f32[64,1024]{1,0:T(8,128)S(1)}, u32[]{:S(2)}, u32[]{:S(2)}) %collective-permute-start) | collective-permute-done | bytes 262176 | tf_op jit(solution)/shard_map/while/body/eval_jaxpr/ppermute | solution.py:28
  461.5 1.9 collective-permute-start
  463.5 6.7 %collective-permute-done = f32[64,1024]{1,0:T(8,128)S(1)} collective-permute-done((f32[64,1024]{1,0:T(8,128)S(1)}, f32[64,1024]{1,0:T(8,128)S(1)}, u32[]{:S(2)}, u32[]{:S(2)}) %collective-permute-start) | collective-permute-done | bytes 262176 | tf_op jit(solution)/shard_map/while/body/eval_jaxpr/ppermute | solution.py:28
  470.6 1.9 collective-permute-start
  472.5 6.7 %collective-permute-done = f32[64,1024]{1,0:T(8,128)S(1)} collective-permute-done((f32[64,1024]{1,0:T(8,128)S(1)}, f32[64,1024]{1,0:T(8,128)S(1)}, u32[]{:S(2)}, u32[]{:S(2)}) %collective-permute-start) | collective-permute-done | bytes 262176 | tf_op jit(solution)/shard_map/while/body/eval_jaxpr/ppermute | solution.py:28
  479.6 1.9 collective-permute-start
  481.5 6.7 %collective-permute-done = f32[64,1024]{1,0:T(8,128)S(1)} collective-permute-done((f32[64,1024]{1,0:T(8,128)S(1)}, f32[64,1024]{1,0:T(8,128)S(1)}, u32[]{:S(2)}, u32[]{:S(2)}) %collective-permute-start) | collective-permute-done | bytes 262176 | tf_op jit(solution)/shard_map/while/body/eval_jaxpr/ppermute | solution.py:28
  488.2 1.1 fusion.10
  (192 shorter events, 25.0 us)
Async XLA Ops:
  0.0 9.4 %copy-start = (f32[64,64]{1,0:T(8,128)S(1)}, f32[64,64]{1,0:T(8,128)}, u32[]{:S(2)}) copy-start(f32[64,64]{1,0:T(8,128)} %param.18) | copy-start | bytes 49156
  0.0 9.9 %copy-start.24 = (s32[6]{0:T(128)S(1)}, s32[6]{0:T(128)}, u32[]{:S(2)}) copy-start(s32[6]{0:T(128)} %constant.100) | copy-start | bytes 76
  0.0 9.0 %copy-start.1 = (f32[1,64,1024]{2,1,0:T(8,128)S(1)}, f32[1,64,1024]{2,1,0:T(8,128)}, u32[]{:S(2)}) copy-start(f32[1,64,1024]{2,1,0:T(8,128)} %param.17) | copy-start | bytes 786436
  0.0 9.3 %copy-start.10 = (s32[6,1024]{1,0:T(8,128)S(1)}, s32[6,1024]{1,0:T(8,128)}, u32[]{:S(2)}) copy-start(s32[6,1024]{1,0:T(8,128)} %param.21) | copy-start | bytes 73732
  0.0 9.4 %copy-start.11 = (s32[6,1024]{1,0:T(8,128)S(1)}, s32[6,1024]{1,0:T(8,128)}, u32[]{:S(2)}) copy-start(s32[6,1024]{1,0:T(8,128)} %param.22) | copy-start | bytes 73732
  1.4 8.6 %copy-start.17 = (pred[512]{0:T(512)(128)(4,1)}, pred[512]{0:T(512)(128)(4,1)S(1)}, u32[]{:S(2)}) copy-start(pred[512]{0:T(512)(128)(4,1)S(1)} %compare_and_fusion.1) | copy-start | bytes 1540
  4.1 6.0 %copy-start.14 = (s32[1024]{0:T(1024)}, s32[1024]{0:T(1024)S(1)}, u32[]{:S(2)}) copy-start(s32[1024]{0:T(1024)S(1)} %get-tuple-element.92) | copy-start | bytes 12292
  4.1 119.4 %copy-start.12 = (s32[1024]{0:T(1024)}, s32[1024]{0:T(1024)S(1)}, u32[]{:S(2)}) copy-start(s32[1024]{0:T(1024)S(1)} %get-tuple-element.91) | copy-start | bytes 12292
  5.3 7.2 %collective-permute-start.1 = (f32[1,16,512]{1,2,0:T(8,128)S(1)}, f32[1,16,512]{1,2,0:T(8,128)S(1)}, u32[]{:S(2)}, u32[]{:S(2)}) collective-permute-start(f32[1,16,512]{1,2,0:T(8,128)S(1)} %select_bitcast_fusion.8), channel_id=1, source_target_pairs={{0,1},{1,0},{2,3},{3,2},{4,5},{5,4},{6,7},{7,6},{8,9},{9,8},{10,11... | collective-permute-start | bytes 98312 | tf_op jit(solution)/shard_map/ppermute | solution.py:19
  7.2 2.9 copy-start.20
  8.6 9.6 %collective-permute-start.2 = (f32[1,16,512]{1,2,0:T(8,128)S(1)}, f32[1,16,512]{1,2,0:T(8,128)}, u32[]{:S(2)}, u32[]{:S(2)}) collective-permute-start(f32[1,16,512]{1,2,0:T(8,128)S(1)} %select_bitcast_fusion.7), channel_id=1, source_target_pairs={{1,0},{0,1},{3,2},{2,3},{5,4},{4,5},{7,6},{6,7},{9,8},{8,9},{11,10... | collective-permute-start | bytes 98312 | tf_op jit(solution)/shard_map/ppermute | solution.py:20
  9.5 110.8 %copy-start.4 = (pred[6,1024]{1,0:T(8,128)(4,1)}, pred[6,1024]{1,0:T(8,128)(4,1)S(1)}, u32[]{:S(2)}) copy-start(pred[6,1024]{1,0:T(8,128)(4,1)S(1)} %get-tuple-element.89) | copy-start | bytes 18436
  9.5 110.8 %copy-start.7 = (pred[6,1024]{1,0:T(8,128)(4,1)}, pred[6,1024]{1,0:T(8,128)(4,1)S(1)}, u32[]{:S(2)}) copy-start(pred[6,1024]{1,0:T(8,128)(4,1)S(1)} %get-tuple-element.90) | copy-start | bytes 18436
  9.9 2.6 copy-start.23
  120.2 0.8 copy-start.3
  120.6 3.9 copy-start.21
  121.0 5.1 %copy-start.15 = (s32[1024]{0:T(1024)S(1)}, s32[1024]{0:T(1024)}, u32[]{:S(2)}) copy-start(s32[1024]{0:T(1024)} %copy-done.14) | copy-start | bytes 12292
  121.1 6.2 %copy-start.18 = (pred[512]{0:T(512)(128)(4,1)S(1)}, pred[512]{0:T(512)(128)(4,1)}, u32[]{:S(2)}) copy-start(pred[512]{0:T(512)(128)(4,1)} %copy-done.17) | copy-start | bytes 1540
  124.7 6.4 %collective-permute-start.4 = (f32[1,16,512]{1,2,0:T(8,128)S(1)}, f32[1,16,512]{1,2,0:T(8,128)}, u32[]{:S(2)}, u32[]{:S(2)}) collective-permute-start(f32[1,16,512]{1,2,0:T(8,128)S(1)} %select_bitcast_fusion.5), channel_id=1, source_target_pairs={{1,0},{0,1},{3,2},{2,3},{5,4},{4,5},{7,6},{6,7},{9,8},{8,9},{11,10... | collective-permute-start | bytes 98312 | tf_op jit(solution)/shard_map/ppermute | solution.py:20
  127.4 9.2 %collective-permute-start.3 = (f32[1,16,512]{1,2,0:T(8,128)S(1)}, f32[1,16,512]{1,2,0:T(8,128)S(1)}, u32[]{:S(2)}, u32[]{:S(2)}) collective-permute-start(f32[1,16,512]{1,2,0:T(8,128)S(1)} %select_bitcast_fusion.6), channel_id=1, source_target_pairs={{0,1},{1,0},{2,3},{3,2},{4,5},{5,4},{6,7},{7,6},{8,9},{9,8},{10,11... | collective-permute-start | bytes 98312 | tf_op jit(solution)/shard_map/ppermute | solution.py:19
  234.9 3.0 copy-start.5
  234.9 3.0 copy-start.8
  238.2 2.2 copy-start.16
  238.2 3.2 copy-start.19
  238.6 4.5 copy-start.13
  238.7 5.5 %copy-start.22 = (pred[512]{0:T(512)(128)(4,1)S(1)}, pred[512]{0:T(512)(128)(4,1)}, u32[]{:S(2)}) copy-start(pred[512]{0:T(512)(128)(4,1)} %copy-done.20) | copy-start | bytes 1540
  241.6 5.4 %collective-permute-start.5 = (f32[1,16,512]{1,2,0:T(8,128)S(1)}, f32[1,16,512]{1,2,0:T(8,128)}, u32[]{:S(2)}, u32[]{:S(2)}) collective-permute-start(f32[1,16,512]{1,2,0:T(8,128)S(1)} %select_bitcast_fusion.4), channel_id=1, source_target_pairs={{0,1},{1,0},{2,3},{3,2},{4,5},{5,4},{6,7},{7,6},{8,9},{9,8},{10,11... | collective-permute-start | bytes 98312 | tf_op jit(solution)/shard_map/ppermute | solution.py:19
  244.3 8.4 %collective-permute-start.6 = (f32[1,16,512]{1,2,0:T(8,128)S(1)}, f32[1,16,512]{1,2,0:T(8,128)S(1)}, u32[]{:S(2)}, u32[]{:S(2)}) collective-permute-start(f32[1,16,512]{1,2,0:T(8,128)S(1)} %select_bitcast_fusion.3), channel_id=1, source_target_pairs={{1,0},{0,1},{3,2},{2,3},{5,4},{4,5},{7,6},{6,7},{9,8},{8,9},{11,10... | collective-permute-start | bytes 98312 | tf_op jit(solution)/shard_map/ppermute | solution.py:20
  351.1 2.8 copy-start.6
  351.1 2.8 copy-start.9
  353.8 1.2 copy-start.2
  355.8 9.6 %collective-permute-start = (f32[64,1024]{1,0:T(8,128)S(1)}, f32[64,1024]{1,0:T(8,128)S(1)}, u32[]{:S(2)}, u32[]{:S(2)}) collective-permute-start(f32[64,1024]{1,0:T(8,128)S(1)} %convolution_add_fusion.4), channel_id=1, source_target_pairs={{0,2},{2,4},{4,6},{6,8},{8,10},{10,12},{12,14},{14,16},{16,18},{18... | collective-permute-start | bytes 786440 | tf_op jit(solution)/shard_map/while/body/eval_jaxpr/ppermute | solution.py:28
  365.8 7.7 %collective-permute-start = (f32[64,1024]{1,0:T(8,128)S(1)}, f32[64,1024]{1,0:T(8,128)S(1)}, u32[]{:S(2)}, u32[]{:S(2)}) collective-permute-start(f32[64,1024]{1,0:T(8,128)S(1)} %convolution_add_fusion.4), channel_id=1, source_target_pairs={{0,2},{2,4},{4,6},{6,8},{8,10},{10,12},{12,14},{14,16},{16,18},{18... | collective-permute-start | bytes 786440 | tf_op jit(solution)/shard_map/while/body/eval_jaxpr/ppermute | solution.py:28
  373.9 7.7 %collective-permute-start = (f32[64,1024]{1,0:T(8,128)S(1)}, f32[64,1024]{1,0:T(8,128)S(1)}, u32[]{:S(2)}, u32[]{:S(2)}) collective-permute-start(f32[64,1024]{1,0:T(8,128)S(1)} %convolution_add_fusion.4), channel_id=1, source_target_pairs={{0,2},{2,4},{4,6},{6,8},{8,10},{10,12},{12,14},{14,16},{16,18},{18... | collective-permute-start | bytes 786440 | tf_op jit(solution)/shard_map/while/body/eval_jaxpr/ppermute | solution.py:28
  382.1 7.7 %collective-permute-start = (f32[64,1024]{1,0:T(8,128)S(1)}, f32[64,1024]{1,0:T(8,128)S(1)}, u32[]{:S(2)}, u32[]{:S(2)}) collective-permute-start(f32[64,1024]{1,0:T(8,128)S(1)} %convolution_add_fusion.4), channel_id=1, source_target_pairs={{0,2},{2,4},{4,6},{6,8},{8,10},{10,12},{12,14},{14,16},{16,18},{18... | collective-permute-start | bytes 786440 | tf_op jit(solution)/shard_map/while/body/eval_jaxpr/ppermute | solution.py:28
  390.2 7.9 %collective-permute-start = (f32[64,1024]{1,0:T(8,128)S(1)}, f32[64,1024]{1,0:T(8,128)S(1)}, u32[]{:S(2)}, u32[]{:S(2)}) collective-permute-start(f32[64,1024]{1,0:T(8,128)S(1)} %convolution_add_fusion.4), channel_id=1, source_target_pairs={{0,2},{2,4},{4,6},{6,8},{8,10},{10,12},{12,14},{14,16},{16,18},{18... | collective-permute-start | bytes 786440 | tf_op jit(solution)/shard_map/while/body/eval_jaxpr/ppermute | solution.py:28
  398.5 8.6 %collective-permute-start = (f32[64,1024]{1,0:T(8,128)S(1)}, f32[64,1024]{1,0:T(8,128)S(1)}, u32[]{:S(2)}, u32[]{:S(2)}) collective-permute-start(f32[64,1024]{1,0:T(8,128)S(1)} %convolution_add_fusion.4), channel_id=1, source_target_pairs={{0,2},{2,4},{4,6},{6,8},{8,10},{10,12},{12,14},{14,16},{16,18},{18... | collective-permute-start | bytes 786440 | tf_op jit(solution)/shard_map/while/body/eval_jaxpr/ppermute | solution.py:28
  407.5 8.6 %collective-permute-start = (f32[64,1024]{1,0:T(8,128)S(1)}, f32[64,1024]{1,0:T(8,128)S(1)}, u32[]{:S(2)}, u32[]{:S(2)}) collective-permute-start(f32[64,1024]{1,0:T(8,128)S(1)} %convolution_add_fusion.4), channel_id=1, source_target_pairs={{0,2},{2,4},{4,6},{6,8},{8,10},{10,12},{12,14},{14,16},{16,18},{18... | collective-permute-start | bytes 786440 | tf_op jit(solution)/shard_map/while/body/eval_jaxpr/ppermute | solution.py:28
  416.5 8.6 %collective-permute-start = (f32[64,1024]{1,0:T(8,128)S(1)}, f32[64,1024]{1,0:T(8,128)S(1)}, u32[]{:S(2)}, u32[]{:S(2)}) collective-permute-start(f32[64,1024]{1,0:T(8,128)S(1)} %convolution_add_fusion.4), channel_id=1, source_target_pairs={{0,2},{2,4},{4,6},{6,8},{8,10},{10,12},{12,14},{14,16},{16,18},{18... | collective-permute-start | bytes 786440 | tf_op jit(solution)/shard_map/while/body/eval_jaxpr/ppermute | solution.py:28
  425.5 8.6 %collective-permute-start = (f32[64,1024]{1,0:T(8,128)S(1)}, f32[64,1024]{1,0:T(8,128)S(1)}, u32[]{:S(2)}, u32[]{:S(2)}) collective-permute-start(f32[64,1024]{1,0:T(8,128)S(1)} %convolution_add_fusion.4), channel_id=1, source_target_pairs={{0,2},{2,4},{4,6},{6,8},{8,10},{10,12},{12,14},{14,16},{16,18},{18... | collective-permute-start | bytes 786440 | tf_op jit(solution)/shard_map/while/body/eval_jaxpr/ppermute | solution.py:28
  434.5 8.6 %collective-permute-start = (f32[64,1024]{1,0:T(8,128)S(1)}, f32[64,1024]{1,0:T(8,128)S(1)}, u32[]{:S(2)}, u32[]{:S(2)}) collective-permute-start(f32[64,1024]{1,0:T(8,128)S(1)} %convolution_add_fusion.4), channel_id=1, source_target_pairs={{0,2},{2,4},{4,6},{6,8},{8,10},{10,12},{12,14},{14,16},{16,18},{18... | collective-permute-start | bytes 786440 | tf_op jit(solution)/shard_map/while/body/eval_jaxpr/ppermute | solution.py:28
  443.5 8.6 %collective-permute-start = (f32[64,1024]{1,0:T(8,128)S(1)}, f32[64,1024]{1,0:T(8,128)S(1)}, u32[]{:S(2)}, u32[]{:S(2)}) collective-permute-start(f32[64,1024]{1,0:T(8,128)S(1)} %convolution_add_fusion.4), channel_id=1, source_target_pairs={{0,2},{2,4},{4,6},{6,8},{8,10},{10,12},{12,14},{14,16},{16,18},{18... | collective-permute-start | bytes 786440 | tf_op jit(solution)/shard_map/while/body/eval_jaxpr/ppermute | solution.py:28
  452.5 8.6 %collective-permute-start = (f32[64,1024]{1,0:T(8,128)S(1)}, f32[64,1024]{1,0:T(8,128)S(1)}, u32[]{:S(2)}, u32[]{:S(2)}) collective-permute-start(f32[64,1024]{1,0:T(8,128)S(1)} %convolution_add_fusion.4), channel_id=1, source_target_pairs={{0,2},{2,4},{4,6},{6,8},{8,10},{10,12},{12,14},{14,16},{16,18},{18... | collective-permute-start | bytes 786440 | tf_op jit(solution)/shard_map/while/body/eval_jaxpr/ppermute | solution.py:28
  461.5 8.6 %collective-permute-start = (f32[64,1024]{1,0:T(8,128)S(1)}, f32[64,1024]{1,0:T(8,128)S(1)}, u32[]{:S(2)}, u32[]{:S(2)}) collective-permute-start(f32[64,1024]{1,0:T(8,128)S(1)} %convolution_add_fusion.4), channel_id=1, source_target_pairs={{0,2},{2,4},{4,6},{6,8},{8,10},{10,12},{12,14},{14,16},{16,18},{18... | collective-permute-start | bytes 786440 | tf_op jit(solution)/shard_map/while/body/eval_jaxpr/ppermute | solution.py:28
  470.6 8.6 %collective-permute-start = (f32[64,1024]{1,0:T(8,128)S(1)}, f32[64,1024]{1,0:T(8,128)S(1)}, u32[]{:S(2)}, u32[]{:S(2)}) collective-permute-start(f32[64,1024]{1,0:T(8,128)S(1)} %convolution_add_fusion.4), channel_id=1, source_target_pairs={{0,2},{2,4},{4,6},{6,8},{8,10},{10,12},{12,14},{14,16},{16,18},{18... | collective-permute-start | bytes 786440 | tf_op jit(solution)/shard_map/while/body/eval_jaxpr/ppermute | solution.py:28
  479.6 8.6 %collective-permute-start = (f32[64,1024]{1,0:T(8,128)S(1)}, f32[64,1024]{1,0:T(8,128)S(1)}, u32[]{:S(2)}, u32[]{:S(2)}) collective-permute-start(f32[64,1024]{1,0:T(8,128)S(1)} %convolution_add_fusion.4), channel_id=1, source_target_pairs={{0,2},{2,4},{4,6},{6,8},{8,10},{10,12},{12,14},{14,16},{16,18},{18... | collective-permute-start | bytes 786440 | tf_op jit(solution)/shard_map/while/body/eval_jaxpr/ppermute | solution.py:28
where the time goes:
time: 497 us; the launch traced here: 489 us
  local copies, waits for them, and re-layouts  312 us (63%)
  waiting for transfers between devices  95.4 us (19%)
  starting transfers between devices  52.2 us (11%)
  other arithmetic  19.2 us (4%)
  matrix products  9.23 us (2%)
    gather x4, local copies, waits for them, and re-layouts, fine_step(): jnp.take_along_axis(extended, neighbor[:, None, :], axis=2)  268 us
    ppermute x15, waiting for transfers between devices, from_behind(): return lax.ppermute(shard, axis, pairs)  79 us
    ppermute x15, starting transfers between devices, from_behind(): return lax.ppermute(shard, axis, pairs)  47.4 us
    select_n x3, other arithmetic, fine_step(): jnp.take_along_axis(extended, neighbor[:, None, :], axis=2)  14 us
    concatenate x3, local copies, waits for them, and re-layouts, fine_step(): jnp.concatenate([opposite, jnp.broadcast_to(halo_part[None], (6, 16, boun...  12 us
    ppermute x3, waiting for transfers between devices, with_halo(): after = lax.ppermute(initial, axis, down)  10.3 us
  transfers between devices with their start and end apart: 21, of which 20 were waited for; matrix products, arithmetic and copies ran while one was open for 3% of the time, Pallas kernels for 0%

commit v1 on v0

v1 whole, which is shorter than its diff:
```python
import functools

import jax
import jax.numpy as jnp
from jax import lax
from jax.experimental import pallas as pl
from jax.experimental.pallas import tpu as pltpu
from jax.sharding import PartitionSpec as P

STEPS = 3
GROUP = 4
LANES = 128
WIDE = 256
MESH = pl.DeviceIdType.MESH

time_step = 0.05


def exact(a, b):
    return jnp.dot(a, b, precision=lax.Precision.HIGHEST, preferred_element_type=jnp.float32)


def parts_of(value):
    head = value.astype(jnp.bfloat16)
    tail = (value - head.astype(jnp.float32)).astype(jnp.bfloat16)
    return head, tail


def keep_split(ref, value):
    rows = value.shape[0]
    head, tail = parts_of(value)
    ref[0:rows, :] = head
    ref[rows : 2 * rows, :] = tail


def split_dot(ref, value):
    rows = ref.shape[0] // 2
    head, tail = parts_of(value)
    both = jnp.dot(ref[...], head, preferred_element_type=jnp.float32)
    rest = jnp.dot(ref[0:rows, :], tail, preferred_element_type=jnp.float32)
    return both[:rows] + (both[rows:] + rest)


def along(value, index, axis):
    return jnp.take_along_axis(value, index, axis=axis, mode="promise_in_bounds")


def pick(sources, index):
    lane = index & (LANES - 1)
    tile = index >> 7
    upper = lower = None
    for number, load in sources:
        first, second = load()
        first, second = along(first, lane, 1), along(second, lane, 1)
        if upper is None:
            upper, lower = first, second
        else:
            here = tile == number
            upper, lower = jnp.where(here, first, upper), jnp.where(here, second, lower)
    return upper, lower


def selection():
    row = lax.broadcasted_iota(jnp.int32, (96, 64), 0)
    node = lax.broadcasted_iota(jnp.int32, (96, 64), 1)
    face, a, b = row >> 4, (row >> 2) & 3, row & 3
    place = jnp.where(
        face < 2, 4 * a + b, jnp.where(face < 4, 16 * a + b, 16 * a + 4 * b)
    ) + jnp.where(face == 1, 48, jnp.where(face == 3, 12, jnp.where(face == 5, 3, 0)))
    return jnp.where(place == node, 1.0, 0.0).astype(jnp.float32)


def kernel(
    n_time, n_space,
    start_ref, stiff_ref, lift_ref, coarse_ref, near_ref, turn_ref, low_ref, high_ref,
    out_ref,
    stack, trace, spot, coarse_start, leave, halo, joined, weights, reach, powers, last_power, one_power,
    defect, gathered, prefix, carry, ends, final,
    halo_send, halo_recv, mix_send, mix_recv, chain_send, chain_recv, back_send, back_recv,
):
    elements = start_ref.shape[2]
    tiles = elements // LANES
    bound = low_ref.shape[1]
    bound_tiles = bound // LANES
    quarter = elements // GROUP
    me_t, me_s = lax.axis_index("tm"), lax.axis_index("space")
    group, rank = me_t // GROUP, me_t % GROUP
    first = group * GROUP
    groups = n_time // GROUP
    below, above = (me_s + n_space - 1) % n_space, (me_s + 1) % n_space
    mates = [first + (rank + by) % GROUP for by in range(1, GROUP)]
    following = (me_t + GROUP) % n_time
    previous = (me_t + n_time - GROUP) % n_time

    barrier = pltpu.get_barrier_semaphore()
    for space in (below, above):
        pl.semaphore_signal(barrier, inc=1, device_id=(me_t, space), device_id_type=MESH)
    for time in mates + [following, previous]:
        pl.semaphore_signal(barrier, inc=1, device_id=(time, me_s), device_id_type=MESH)

    def keep_traces(tile):
        for i in range(4):
            trace[tile, 0, 4 * i : 4 * i + 4, :] = stack[tile, 16 * i : 16 * i + 4, :]
            trace[tile, 1, 4 * i : 4 * i + 4, :] = stack[tile, 16 * i + 12 : 16 * i + 16, :]
        trace[tile, 2] = stack[tile, pl.ds(0, 16, stride=4), :]
        trace[tile, 3] = stack[tile, pl.ds(3, 16, stride=4), :]

    for tile in range(tiles):
        stack[tile, 0:64, :] = start_ref[0, :, tile * LANES : (tile + 1) * LANES]

    def local_source(face, s):
        if face == 0:
            return s, lambda: (stack[s, 0:8, :], stack[s, 8:16, :])
        if face == 1:
            return s, lambda: (stack[s, 48:56, :], stack[s, 56:64, :])
        return s, lambda: (trace[s, face - 2, 0:8, :], trace[s, face - 2, 8:16, :])

    def wide_index(ref, row, t):
        at = pl.multiple_of(t * LANES, LANES)
        return jnp.broadcast_to(ref[row : row + 1, pl.ds(at, LANES)], (8, LANES))

    def halo_copies(step):
        return [
            pltpu.make_async_remote_copy(
                src_ref=leave.at[step, side],
                dst_ref=halo.at[step, side],
                send_sem=halo_send.at[step, side],
                recv_sem=halo_recv.at[step, side],
                device_id=(me_t, target),
                device_id_type=MESH,
            )
            for side, target in ((0, below), (1, above))
        ]

    def send_halo(step):
        def fill(t, _):
            for side, ref in ((0, low_ref), (1, high_ref)):
                sources = [local_source(side, s) for s in range(tiles)]
                upper, lower = pick(sources, wide_index(ref, 0, t))
                leave[step, side, t, 0:8, :] = upper
                leave[step, side, t, 8:16, :] = lower
            return 0

        lax.fori_loop(0, bound_tiles, fill, 0)
        if step == 0:
            pl.semaphore_wait(barrier, 2 + GROUP - 1 + 2)
        copies = halo_copies(step)
        for copy in copies:
            copy.start()
        return copies

    def place(face, t, upper, lower):
        for half in range(2):
            index = spot[face, t, 8 * half : 8 * half + 8, :]
            row = index & 7
            turned = jnp.where(index < 8, along(upper, row, 0), along(lower, row, 0))
            at = 64 + 16 * face + 8 * half
            stack[t, at : at + 8, :] = turned

    def inner_faces(t, _):
        for face in range(2, 6):
            sources = [local_source(face ^ 1, s) for s in range(tiles)]
            place(face, t, *pick(sources, wide_index(near_ref, face, t)))
        return 0

    def outer_faces(step):
        def body(t, _):
            for face in range(2):
                side = 1 - face
                sources = [local_source(face ^ 1, s) for s in range(tiles)]
                for b in range(bound_tiles):
                    number = tiles + face * bound_tiles + b
                    sources.append(
                        (
                            number,
                            lambda b=b: (
                                halo[step, side, b, 0:8, :],
                                halo[step, side, b, 8:16, :],
                            ),
                        )
                    )
                place(face, t, *pick(sources, wide_index(near_ref, face, t)))
            return 0

        return body

    copies = send_halo(0)

    def spots(t, _):
        row = lax.broadcasted_iota(jnp.int32, (16, LANES), 0)
        at = pl.multiple_of(t * LANES, LANES)
        for face in range(6):
            code = jnp.broadcast_to(turn_ref[face : face + 1, pl.ds(at, LANES)], (16, LANES))
            a, b = row >> 2, row & 3
            a = jnp.where((code & 1) != 0, 3 - a, a)
            b = jnp.where((code & 2) != 0, 3 - b, b)
            spot[face, t] = jnp.where((code & 4) != 0, 4 * b + a, 4 * a + b)
        return 0

    lax.fori_loop(0, tiles, spots, 0)
    for tile in range(tiles):
        keep_traces(tile)
    lifting = lift_ref[...]
    row64 = lax.broadcasted_iota(jnp.int32, (64, 64), 0)
    col64 = lax.broadcasted_iota(jnp.int32, (64, 64), 1)
    unit = jnp.where(row64 == col64, 1.0, 0.0).astype(jnp.float32)
    joined[:, 0:64] = stiff_ref[...] - exact(lifting, selection()) + unit
    joined[:, 64:160] = lifting
    keep_split(weights, joined[...])
    one = coarse_ref[...]
    two = exact(one, one)
    three = exact(two, one)
    four = exact(two, two)
    keep_split(one_power, one)
    keep_split(last_power, four)
    for part in range(2):
        for at, power in enumerate((one, two, three)):
            value = parts_of(power)[part]
            powers[192 * part + 64 * at : 192 * part + 64 * at + 64, :] = value
    zero = jnp.zeros((64, 64), jnp.float32)
    table = ((one, zero, zero), (two, one, zero), (three, two, one))
    for i in range(3):
        line = jnp.concatenate(table[i], axis=1)
        head, tail = parts_of(line)
        reach[64 * i : 64 * i + 64, :] = head
        reach[192 + 64 * i : 256 + 64 * i, :] = tail
    for c in range(elements // WIDE):
        columns = start_ref[0, :, c * WIDE : (c + 1) * WIDE]
        coarse_start[c] = jnp.where(me_t == 0, 0.0, split_dot(one_power, columns))

    for step in range(STEPS):
        if step > 0:
            copies = send_halo(step)
            for tile in range(tiles):
                keep_traces(tile)
        lax.fori_loop(0, tiles, inner_faces, 0)
        for copy in copies:
            copy.wait()
        lax.fori_loop(0, tiles, outer_faces(step), 0)
        for c in range(elements // WIDE):
            operand = jnp.concatenate([stack[2 * c], stack[2 * c + 1]], axis=1)
            state = operand[0:64]
            rate = split_dot(weights, operand) - state * state * state
            later = state + time_step * rate
            if step < STEPS - 1:
                stack[2 * c, 0:64, :] = later[:, :LANES]
                stack[2 * c + 1, 0:64, :] = later[:, LANES:]
            else:
                q, at = c * WIDE // quarter, c * WIDE % quarter
                defect[q, :, at : at + WIDE] = later - coarse_start[c]

    def exchange(source, target, send, recv):
        out = []
        for by in range(1, GROUP):
            other = (rank + by) % GROUP
            out.append(
                pltpu.make_async_remote_copy(
                    src_ref=source.at[other],
                    dst_ref=target.at[rank],
                    send_sem=send.at[by - 1],
                    recv_sem=recv.at[by - 1],
                    device_id=(first + other, me_s),
                    device_id_type=MESH,
                )
            )
        for copy in out:
            copy.start()
        target[rank] = source[rank]
        for copy in out:
            copy.wait()

    exchange(defect, gathered, mix_send, mix_recv)
    inputs = jnp.concatenate([gathered[0], gathered[1], gathered[2]], axis=0)
    reached = split_dot(reach, inputs)
    prefix[0] = gathered[0]
    for m in range(1, GROUP):
        prefix[m] = gathered[m] + reached[64 * m - 64 : 64 * m]

    chain = pltpu.make_async_remote_copy(
        src_ref=ends.at[GROUP - 1],
        dst_ref=carry,
        send_sem=chain_send,
        recv_sem=chain_recv,
        device_id=(following, me_s),
        device_id_type=MESH,
    )

    @pl.when(group == 0)
    def _():
        carry[...] = jnp.zeros_like(carry)

    @pl.when(group > 0)
    def _():
        chain.wait_recv()

    ends[GROUP - 1] = prefix[GROUP - 1] + split_dot(last_power, carry[...])

    @pl.when(group < groups - 1)
    def _():
        chain.start()

    spread = split_dot(powers, carry[...])
    for m in range(GROUP - 1):
        ends[m] = prefix[m] + spread[64 * m : 64 * m + 64]
    exchange(ends, final, back_send, back_recv)

    @pl.when(group < groups - 1)
    def _():
        chain.wait_send()

    for q in range(GROUP):
        out_ref[0, :, q * quarter : (q + 1) * quarter] = final[q]


def shards(start_state, stiffness, lifting, coarse, neighbor, orientation, send_low, send_high):
    elements = start_state.shape[2]
    bound = send_low.shape[0]
    tiles, bound_tiles, quarter = elements // LANES, bound // LANES, elements // GROUP
    f32, b16, i32 = jnp.float32, jnp.bfloat16, jnp.int32
    dma = pltpu.SemaphoreType.DMA
    vmem = pl.BlockSpec(memory_space=pltpu.VMEM)
    return pl.pallas_call(
        functools.partial(kernel, lax.axis_size("tm"), lax.axis_size("space")),
        out_shape=jax.ShapeDtypeStruct(start_state.shape, f32),
        in_specs=[vmem] * 8,
        out_specs=vmem,
        scratch_shapes=[
            pltpu.VMEM((tiles, 160, LANES), f32),
            pltpu.VMEM((tiles, 4, 16, LANES), f32),
            pltpu.VMEM((6, tiles, 16, LANES), i32),
            pltpu.VMEM((elements // WIDE, 64, WIDE), f32),
            pltpu.VMEM((STEPS, 2, bound_tiles, 16, LANES), f32),
            pltpu.VMEM((STEPS, 2, bound_tiles, 16, LANES), f32),
            pltpu.VMEM((64, 160), f32),
            pltpu.VMEM((128, 160), b16),
            pltpu.VMEM((384, 192), b16),
            pltpu.VMEM((384, 64), b16),
            pltpu.VMEM((128, 64), b16),
            pltpu.VMEM((128, 64), b16),
            pltpu.VMEM((GROUP, 64, quarter), f32),
            pltpu.VMEM((GROUP, 64, quarter), f32),
            pltpu.VMEM((GROUP, 64, quarter), f32),
            pltpu.VMEM((64, quarter), f32),
            pltpu.VMEM((GROUP, 64, quarter), f32),
            pltpu.VMEM((GROUP, 64, quarter), f32),
            dma((STEPS, 2)),
            dma((STEPS, 2)),
            dma((GROUP - 1,)),
            dma((GROUP - 1,)),
            dma,
            dma,
            dma((GROUP - 1,)),
            dma((GROUP - 1,)),
        ],
        compiler_params=pltpu.CompilerParams(
            collective_id=0, has_side_effects=True, vmem_limit_bytes=40 * 1024 * 1024
        ),
    )(
        start_state, stiffness, lifting, coarse, neighbor, orientation,
        send_low.reshape(1, bound), send_high.reshape(1, bound),
    )


def solution(mesh):
    return jax.shard_map(
        shards,
        mesh=mesh,
        in_specs=(
            P("tm", None, "space"),
            P(),
            P(),
            P(),
            P(None, "space"),
            P(None, "space"),
            P("space"),
            P("space"),
        ),
        out_specs=P("tm", None, "space"),
        check_vma=False,
    )
```

time: 497 us -> 44.8 us (0.09); the launches traced: 489 us -> 44.3 us
  local copies, waits for them, and re-layouts: 312 us -> 6.8 us
  waiting for transfers between devices: 95.4 us -> 0 us
  starting transfers between devices: 52.2 us -> 0 us
  Pallas kernels: 0 us -> 37.4 us
  other arithmetic: 19.2 us -> 0 us
  matrix products: 9.23 us -> 0 us
    gather x13 -> x0, local copies, waits for them, and re-layouts: 277 us -> none  [the longest x4 268 us: fine_step(): jnp.take_along_axis(extended, neighbor[:, None, :], axis=2)]
    ppermute x21 -> x0, waiting for transfers between devices: 95.4 us -> none  [the longest x15 79 us: from_behind(): return lax.ppermute(shard, axis, pairs)]
    ppermute x21 -> x0, starting transfers between devices: 52.2 us -> none  [the longest x15 47.4 us: from_behind(): return lax.ppermute(shard, axis, pairs)]
    pallas_call x0 -> x1, Pallas kernels: none -> 37.4 us  [shards(): pl.pallas_call(functools.partial(kernel, lax.axis_size('tm'), lax.axis_si...]
    select_n x20 -> x0, other arithmetic: 15.9 us -> none  [the longest x3 14 us: fine_step(): jnp.take_along_axis(extended, neighbor[:, None, :], axis=2)]
    concatenate x3 -> x0, local copies, waits for them, and re-layouts: 12 us -> none  [fine_step(): jnp.concatenate([opposite, jnp.broadcast_to(halo_part[None], (6, 16, boun...]
    dot_general x23 -> x0, matrix products: 9.23 us -> none  [product(): jnp.dot(matrix, vector, precision=lax.Precision.HIGHEST, preferred_elemen...]
    select_n x3 -> x0, local copies, waits for them, and re-layouts: 8.34 us -> none  [fine_step(): jnp.take_along_axis(extended, neighbor[:, None, :], axis=2)]
  transfers between devices with their start and end apart: 21 -> 0, of which waited for: 20 -> 0; matrix products, arithmetic and copies ran while one was open for 3% -> 0% of each run, Pallas kernels for 0% -> 0%
where the time goes in v1:
time: 44.8 us; the launch traced here: 44.3 us
  Pallas kernels  37.4 us (83%)
  local copies, waits for them, and re-layouts  6.8 us (15%)
    pallas_call x1, Pallas kernels, shards(): pl.pallas_call(functools.partial(kernel, lax.axis_size('tm'), lax.axis_si...  37.4 us
    unnamed x17, local copies, waits for them, and re-layouts  6.8 us

profile of v1, /device:TPU:25, one launch (start us, length us, event | category | flops | bytes accessed | tf_op | source)
XLA Modules:
  0.0 44.3 jit_solution(13406257031786572016)
XLA Ops:
  0.0 0.0 copy-start.6
  0.0 0.7 %copy-done.6 = s32[512]{0:T(512)S(1)} copy-done((s32[512]{0:T(512)S(1)}, s32[512]{0:T(512)}, u32[]{:S(2)}) %copy-start.6) | copy-done | bytes 2072
  0.7 0.0 copy-start
  0.7 0.9 %copy-done = f32[1,64,1024]{2,1,0:T(8,128)S(1)} copy-done((f32[1,64,1024]{2,1,0:T(8,128)S(1)}, f32[1,64,1024]{2,1,0:T(8,128)}, u32[]{:S(2)}) %copy-start) | copy-done | bytes 262168
  1.6 0.0 copy-start.1
  1.6 0.8 %copy-done.1 = f32[64,64]{1,0:T(8,128)S(1)} copy-done((f32[64,64]{1,0:T(8,128)S(1)}, f32[64,64]{1,0:T(8,128)}, u32[]{:S(2)}) %copy-start.1) | copy-done | bytes 16408
  2.4 0.0 copy-start.2
  2.4 0.8 %copy-done.2 = f32[64,96]{1,0:T(8,128)S(1)} copy-done((f32[64,96]{1,0:T(8,128)S(1)}, f32[64,96]{1,0:T(8,128)}, u32[]{:S(2)}) %copy-start.2) | copy-done | bytes 24600
  3.1 0.0 copy-start.3
  3.2 0.8 %copy-done.3 = f32[64,64]{1,0:T(8,128)S(1)} copy-done((f32[64,64]{1,0:T(8,128)S(1)}, f32[64,64]{1,0:T(8,128)}, u32[]{:S(2)}) %copy-start.3) | copy-done | bytes 16408
  3.9 0.0 copy-start.4
  3.9 0.8 %copy-done.4 = s32[6,1024]{1,0:T(8,128)S(1)} copy-done((s32[6,1024]{1,0:T(8,128)S(1)}, s32[6,1024]{1,0:T(8,128)}, u32[]{:S(2)}) %copy-start.4) | copy-done | bytes 24600
  4.7 0.0 copy-start.5
  4.7 0.8 %copy-done.5 = s32[6,1024]{1,0:T(8,128)S(1)} copy-done((s32[6,1024]{1,0:T(8,128)S(1)}, s32[6,1024]{1,0:T(8,128)}, u32[]{:S(2)}) %copy-start.5) | copy-done | bytes 24600
  5.4 0.0 copy-start.7
  5.4 0.7 %copy-done.7 = s32[512]{0:T(512)S(1)} copy-done((s32[512]{0:T(512)S(1)}, s32[512]{0:T(512)}, u32[]{:S(2)}) %copy-start.7) | copy-done | bytes 2072
  6.1 37.4 %shard_map.82 = f32[1,64,1024]{2,1,0:T(8,128)S(1)} custom-call(f32[1,64,1024]{2,1,0:T(8,128)S(1)} %copy-done, f32[64,64]{1,0:T(8,128)S(1)} %copy-done.1, f32[64,96]{1,0:T(8,128)S(1)} %copy-done.2, f32[64,64]{1,0:T(8,128)S(1)} %copy-done.3, s32[6,1024]{1,0:T(8,128)S(1)} %copy-done.4, s32[6,1024]{1,0:T(8,128)S(1)} %copy-done.5, s32[1,512]{1,0:T(1,128)S(1)} %bitcast.2, ...), custom_call_target="tpu_custom_call" | custom-call | tf_op jit(solution)/shard_map/pallas_call | solution.py:322
  43.5 0.7 %copy.10 = f32[1,64,1024]{2,1,0:T(8,128)} copy(f32[1,64,1024]{2,1,0:T(8,128)S(1)} %shard_map.82) | data formatting | bytes 524288
Async XLA Ops:
  0.0 0.7 %copy-start.6 = (s32[512]{0:T(512)S(1)}, s32[512]{0:T(512)}, u32[]{:S(2)}) copy-start(s32[512]{0:T(512)} %param.14) | copy-start | bytes 6148
  0.7 0.9 %copy-start = (f32[1,64,1024]{2,1,0:T(8,128)S(1)}, f32[1,64,1024]{2,1,0:T(8,128)}, u32[]{:S(2)}) copy-start(f32[1,64,1024]{2,1,0:T(8,128)} %start_ref.1) | copy-start | bytes 786436
  1.6 0.8 %copy-start.1 = (f32[64,64]{1,0:T(8,128)S(1)}, f32[64,64]{1,0:T(8,128)}, u32[]{:S(2)}) copy-start(f32[64,64]{1,0:T(8,128)} %stiff_ref.1) | copy-start | bytes 49156
  2.4 0.8 %copy-start.2 = (f32[64,96]{1,0:T(8,128)S(1)}, f32[64,96]{1,0:T(8,128)}, u32[]{:S(2)}) copy-start(f32[64,96]{1,0:T(8,128)} %lift_ref.1) | copy-start | bytes 73732
  3.1 0.8 %copy-start.3 = (f32[64,64]{1,0:T(8,128)S(1)}, f32[64,64]{1,0:T(8,128)}, u32[]{:S(2)}) copy-start(f32[64,64]{1,0:T(8,128)} %coarse_ref.1) | copy-start | bytes 49156
  3.9 0.8 %copy-start.4 = (s32[6,1024]{1,0:T(8,128)S(1)}, s32[6,1024]{1,0:T(8,128)}, u32[]{:S(2)}) copy-start(s32[6,1024]{1,0:T(8,128)} %near_ref.1) | copy-start | bytes 73732
  4.7 0.8 %copy-start.5 = (s32[6,1024]{1,0:T(8,128)S(1)}, s32[6,1024]{1,0:T(8,128)}, u32[]{:S(2)}) copy-start(s32[6,1024]{1,0:T(8,128)} %turn_ref.1) | copy-start | bytes 73732
  5.4 0.7 %copy-start.7 = (s32[512]{0:T(512)S(1)}, s32[512]{0:T(512)}, u32[]{:S(2)}) copy-start(s32[512]{0:T(512)} %param.15) | copy-start | bytes 6148

commit v2 on v1

--- a/solution.py
+++ b/solution.py
@@ -75,10 +75,39 @@
     start_ref, stiff_ref, lift_ref, coarse_ref, near_ref, turn_ref, low_ref, high_ref,
     out_ref,
     stack, trace, spot, coarse_start, leave, halo, joined, weights, reach, powers, last_power, one_power,
-    defect, gathered, prefix, carry, ends, final,
+    defect, gathered, carry, ends, final,
+    start_in, stiff_in, lift_in, coarse_in, near_in, turn_in, low_in, high_in, load_sem, state_sem,
     halo_send, halo_recv, mix_send, mix_recv, chain_send, chain_recv, back_send, back_recv,
 ):
     elements = start_ref.shape[2]
+    loads = {}
+    for number, (name, source, target) in enumerate(
+        (
+            ("low", low_ref, low_in),
+            ("high", high_ref, high_in),
+            ("turn", turn_ref, turn_in),
+            ("stiff", stiff_ref, stiff_in),
+            ("lift", lift_ref, lift_in),
+            ("near", near_ref, near_in),
+            ("coarse", coarse_ref, coarse_in),
+            ("start", start_ref, start_in),
+        )
+    ):
+        loads[name] = pltpu.make_async_copy(source, target, load_sem.at[number])
+    for name in ("low", "high"):
+        loads[name].start()
+    states = []
+    for tile in range(elements // LANES):
+        states.append(
+            pltpu.make_async_copy(
+                start_ref.at[0, :, tile * LANES : (tile + 1) * LANES],
+                stack.at[tile, 0:64, :],
+                state_sem.at[tile],
+            )
+        )
+        states[-1].start()
+    for name in ("turn", "stiff", "lift", "near", "coarse", "start"):
+        loads[name].start()
     tiles = elements // LANES
     bound = low_ref.shape[1]
     bound_tiles = bound // LANES
@@ -105,8 +134,10 @@
         trace[tile, 2] = stack[tile, pl.ds(0, 16, stride=4), :]
         trace[tile, 3] = stack[tile, pl.ds(3, 16, stride=4), :]
 
-    for tile in range(tiles):
-        stack[tile, 0:64, :] = start_ref[0, :, tile * LANES : (tile + 1) * LANES]
+    loads["low"].wait()
+    loads["high"].wait()
+    for copy in states:
+        copy.wait()
 
     def local_source(face, s):
         if face == 0:
@@ -134,14 +165,14 @@
 
     def send_halo(step):
         def fill(t, _):
-            for side, ref in ((0, low_ref), (1, high_ref)):
+            for side, ref in ((0, low_in), (1, high_in)):
                 sources = [local_source(side, s) for s in range(tiles)]
                 upper, lower = pick(sources, wide_index(ref, 0, t))
                 leave[step, side, t, 0:8, :] = upper
                 leave[step, side, t, 8:16, :] = lower
             return 0
 
-        lax.fori_loop(0, bound_tiles, fill, 0)
+        lax.fori_loop(0, bound_tiles, fill, 0, unroll=4)
         if step == 0:
             pl.semaphore_wait(barrier, 2 + GROUP - 1 + 2)
         copies = halo_copies(step)
@@ -160,7 +191,7 @@
     def inner_faces(t, _):
         for face in range(2, 6):
             sources = [local_source(face ^ 1, s) for s in range(tiles)]
-            place(face, t, *pick(sources, wide_index(near_ref, face, t)))
+            place(face, t, *pick(sources, wide_index(near_in, face, t)))
         return 0
 
     def outer_faces(step):
@@ -179,7 +210,7 @@
                             ),
                         )
                     )
-                place(face, t, *pick(sources, wide_index(near_ref, face, t)))
+                place(face, t, *pick(sources, wide_index(near_in, face, t)))
             return 0
 
         return body
@@ -190,126 +221,178 @@
         row = lax.broadcasted_iota(jnp.int32, (16, LANES), 0)
         at = pl.multiple_of(t * LANES, LANES)
         for face in range(6):
-            code = jnp.broadcast_to(turn_ref[face : face + 1, pl.ds(at, LANES)], (16, LANES))
+            code = jnp.broadcast_to(turn_in[face : face + 1, pl.ds(at, LANES)], (16, LANES))
             a, b = row >> 2, row & 3
             a = jnp.where((code & 1) != 0, 3 - a, a)
             b = jnp.where((code & 2) != 0, 3 - b, b)
             spot[face, t] = jnp.where((code & 4) != 0, 4 * b + a, 4 * a + b)
         return 0
 
+    loads["turn"].wait()
     lax.fori_loop(0, tiles, spots, 0)
     for tile in range(tiles):
         keep_traces(tile)
-    lifting = lift_ref[...]
-    row64 = lax.broadcasted_iota(jnp.int32, (64, 64), 0)
-    col64 = lax.broadcasted_iota(jnp.int32, (64, 64), 1)
-    unit = jnp.where(row64 == col64, 1.0, 0.0).astype(jnp.float32)
-    joined[:, 0:64] = stiff_ref[...] - exact(lifting, selection()) + unit
-    joined[:, 64:160] = lifting
-    keep_split(weights, joined[...])
-    one = coarse_ref[...]
-    two = exact(one, one)
-    three = exact(two, one)
-    four = exact(two, two)
-    keep_split(one_power, one)
-    keep_split(last_power, four)
-    for part in range(2):
-        for at, power in enumerate((one, two, three)):
-            value = parts_of(power)[part]
-            powers[192 * part + 64 * at : 192 * part + 64 * at + 64, :] = value
-    zero = jnp.zeros((64, 64), jnp.float32)
-    table = ((one, zero, zero), (two, one, zero), (three, two, one))
-    for i in range(3):
-        line = jnp.concatenate(table[i], axis=1)
-        head, tail = parts_of(line)
-        reach[64 * i : 64 * i + 64, :] = head
-        reach[192 + 64 * i : 256 + 64 * i, :] = tail
-    for c in range(elements // WIDE):
-        columns = start_ref[0, :, c * WIDE : (c + 1) * WIDE]
-        coarse_start[c] = jnp.where(me_t == 0, 0.0, split_dot(one_power, columns))
+
+    def fine_matrix():
+        loads["stiff"].wait()
+        loads["lift"].wait()
+        lifting = lift_in[...]
+        row64 = lax.broadcasted_iota(jnp.int32, (64, 64), 0)
+        col64 = lax.broadcasted_iota(jnp.int32, (64, 64), 1)
+        unit = jnp.where(row64 == col64, 1.0, 0.0).astype(jnp.float32)
+        joined[:, 0:64] = stiff_in[...] - exact(lifting, selection()) + unit
+        joined[:, 64:160] = lifting
+        keep_split(weights, joined[...])
+
+    def coarse_matrices():
+        loads["coarse"].wait()
+        one = coarse_in[...]
+        two = exact(one, one)
+        three = exact(two, one)
+        four = exact(two, two)
+        keep_split(one_power, one)
+        keep_split(last_power, four)
+        for part in range(2):
+            for at, power in enumerate((one, two, three)):
+                value = parts_of(power)[part]
+                powers[192 * part + 64 * at : 192 * part + 64 * at + 64, :] = value
+        zero = jnp.zeros((64, 64), jnp.float32)
+        table = ((one, zero, zero), (two, one, zero), (three, two, one))
+        for i in range(3):
+            line = jnp.concatenate(table[i], axis=1)
+            head, tail = parts_of(line)
+            reach[64 * i : 64 * i + 64, :] = head
+            reach[192 + 64 * i : 256 + 64 * i, :] = tail
+
+    def coarse_first():
+        loads["start"].wait()
+        for c in range(elements // WIDE):
+            columns = start_in[0, :, c * WIDE : (c + 1) * WIDE]
+            coarse_start[c] = jnp.where(me_t == 0, 0.0, split_dot(one_power, columns))
+
+    def advance(c):
+        operand = jnp.concatenate([stack[2 * c], stack[2 * c + 1]], axis=1)
+        state = operand[0:64]
+        rate = split_dot(weights, operand) - state * state * state
+        return state + time_step * rate
 
     for step in range(STEPS):
         if step > 0:
             copies = send_halo(step)
             for tile in range(tiles):
                 keep_traces(tile)
-        lax.fori_loop(0, tiles, inner_faces, 0)
+        if step == 0:
+            fine_matrix()
+            loads["near"].wait()
+        lax.fori_loop(0, tiles, inner_faces, 0, unroll=4)
+        if step == 1:
+            coarse_matrices()
+        if step == 2:
+            coarse_first()
         for copy in copies:
             copy.wait()
-        lax.fori_loop(0, tiles, outer_faces(step), 0)
-        for c in range(elements // WIDE):
-            operand = jnp.concatenate([stack[2 * c], stack[2 * c + 1]], axis=1)
-            state = operand[0:64]
-            rate = split_dot(weights, operand) - state * state * state
-            later = state + time_step * rate
-            if step < STEPS - 1:
+        lax.fori_loop(0, tiles, outer_faces(step), 0, unroll=4)
+        if step < STEPS - 1:
+            for c in range(elements // WIDE):
+                later = advance(c)
                 stack[2 * c, 0:64, :] = later[:, :LANES]
                 stack[2 * c + 1, 0:64, :] = later[:, LANES:]
-            else:
-                q, at = c * WIDE // quarter, c * WIDE % quarter
-                defect[q, :, at : at + WIDE] = later - coarse_start[c]
-
-    def exchange(source, target, send, recv):
-        out = []
-        for by in range(1, GROUP):
-            other = (rank + by) % GROUP
-            out.append(
-                pltpu.make_async_remote_copy(
-                    src_ref=source.at[other],
-                    dst_ref=target.at[rank],
-                    send_sem=send.at[by - 1],
-                    recv_sem=recv.at[by - 1],
-                    device_id=(first + other, me_s),
-                    device_id_type=MESH,
-                )
-            )
-        for copy in out:
-            copy.start()
-        target[rank] = source[rank]
-        for copy in out:
-            copy.wait()
-
-    exchange(defect, gathered, mix_send, mix_recv)
-    inputs = jnp.concatenate([gathered[0], gathered[1], gathered[2]], axis=0)
-    reached = split_dot(reach, inputs)
-    prefix[0] = gathered[0]
-    for m in range(1, GROUP):
-        prefix[m] = gathered[m] + reached[64 * m - 64 : 64 * m]
-
-    chain = pltpu.make_async_remote_copy(
-        src_ref=ends.at[GROUP - 1],
-        dst_ref=carry,
-        send_sem=chain_send,
-        recv_sem=chain_recv,
-        device_id=(following, me_s),
-        device_id_type=MESH,
-    )
-
-    @pl.when(group == 0)
-    def _():
-        carry[...] = jnp.zeros_like(carry)
+
+    pairs = (None, rank + 1 - 2 * (rank % 2), (rank + 2) % GROUP, GROUP - 1 - rank)
+
+    def swap(source, target, send, recv, by, half):
+        other = pairs[by]
+        return pltpu.make_async_remote_copy(
+            src_ref=source.at[other, half],
+            dst_ref=target.at[rank, half],
+            send_sem=send.at[by - 1, half],
+            recv_sem=recv.at[by - 1, half],
+            device_id=(first + other, me_s),
+            device_id_type=MESH,
+        )
+
+    def last_step(q, target, slot):
+        for w in range(quarter // WIDE):
+            c = q * (quarter // WIDE) + w
+            value = advance(c) - coarse_start[c]
+            for piece in range(2):
+                at = w * WIDE + piece * LANES
+                half, column = at // (quarter // 2), at % (quarter // 2)
+                target[slot, half, :, column : column + LANES] = value[
+                    :, piece * LANES : (piece + 1) * LANES
+                ]
+
+    mixes = {(by, h): swap(defect, gathered, mix_send, mix_recv, by, h) for by in (2, 3, 1) for h in (0, 1)}
+    for by in (2, 3, 1):
+        last_step(pairs[by], defect, pairs[by])
+        mixes[by, 0].start()
+    for by in (2, 3, 1):
+        mixes[by, 1].start()
+    last_step(rank, gathered, rank)
+
+    chain = [
+        pltpu.make_async_remote_copy(
+            src_ref=ends.at[GROUP - 1, h],
+            dst_ref=carry.at[h],
+            send_sem=chain_send.at[h],
+            recv_sem=chain_recv.at[h],
+            device_id=(following, me_s),
+            device_id_type=MESH,
+        )
+        for h in range(2)
+    ]
+    backs = {(by, h): swap(ends, final, back_send, back_recv, by, h) for by in (2, 3, 1) for h in (0, 1)}
+
+    def give_back(h):
+        for by in (2, 3, 1):
+            backs[by, h].start()
+        final[rank, h] = ends[rank, h]
+
+    for h in range(2):
+        for by in (1, 2, 3):
+            mixes[by, h].wait_recv()
+        inputs = jnp.concatenate([gathered[0, h], gathered[1, h], gathered[2, h]], axis=0)
+        reached = split_dot(reach, inputs)
+        ends[0, h] = gathered[0, h]
+        for m in range(1, GROUP):
+            ends[m, h] = gathered[m, h] + reached[64 * m - 64 : 64 * m]
+
+        @pl.when(group == 0)
+        def _():
+            if groups > 1:
+                chain[h].start()
+            give_back(h)
 
     @pl.when(group > 0)
     def _():
-        chain.wait_recv()
-
-    ends[GROUP - 1] = prefix[GROUP - 1] + split_dot(last_power, carry[...])
+        for h in range(2):
+            chain[h].wait_recv()
+            held = carry[h]
+            ends[GROUP - 1, h] = ends[GROUP - 1, h] + split_dot(last_power, held)
+
+            @pl.when(group < groups - 1)
+            def _():
+                chain[h].start()
+
+            spread = split_dot(powers, held)
+            for m in range(GROUP - 1):
+                ends[m, h] = ends[m, h] + spread[64 * m : 64 * m + 64]
+            give_back(h)
+
+    for copy in mixes.values():
+        copy.wait_send()
 
     @pl.when(group < groups - 1)
     def _():
-        chain.start()
-
-    spread = split_dot(powers, carry[...])
-    for m in range(GROUP - 1):
-        ends[m] = prefix[m] + spread[64 * m : 64 * m + 64]
-    exchange(ends, final, back_send, back_recv)
-
-    @pl.when(group < groups - 1)
-    def _():
-        chain.wait_send()
-
-    for q in range(GROUP):
-        out_ref[0, :, q * quarter : (q + 1) * quarter] = final[q]
+        for h in range(2):
+            chain[h].wait_send()
+
+    for h in range(2):
+        for by in (1, 2, 3):
+            backs[by, h].wait()
+        for q in range(GROUP):
+            at = q * quarter + h * (quarter // 2)
+            out_ref[0, :, at : at + quarter // 2] = final[q, h]
 
 
 def shards(start_state, stiffness, lifting, coarse, neighbor, orientation, send_low, send_high):
@@ -322,7 +405,7 @@
     return pl.pallas_call(
         functools.partial(kernel, lax.axis_size("tm"), lax.axis_size("space")),
         out_shape=jax.ShapeDtypeStruct(start_state.shape, f32),
-        in_specs=[vmem] * 8,
+        in_specs=[pl.BlockSpec(memory_space=pltpu.HBM)] * 8,
         out_specs=vmem,
         scratch_shapes=[
             pltpu.VMEM((tiles, 160, LANES), f32),
@@ -337,20 +420,29 @@
             pltpu.VMEM((384, 64), b16),
             pltpu.VMEM((128, 64), b16),
             pltpu.VMEM((128, 64), b16),
-            pltpu.VMEM((GROUP, 64, quarter), f32),
-            pltpu.VMEM((GROUP, 64, quarter), f32),
-            pltpu.VMEM((GROUP, 64, quarter), f32),
-            pltpu.VMEM((64, quarter), f32),
-            pltpu.VMEM((GROUP, 64, quarter), f32),
-            pltpu.VMEM((GROUP, 64, quarter), f32),
+            pltpu.VMEM((GROUP, 2, 64, quarter // 2), f32),
+            pltpu.VMEM((GROUP, 2, 64, quarter // 2), f32),
+            pltpu.VMEM((2, 64, quarter // 2), f32),
+            pltpu.VMEM((GROUP, 2, 64, quarter // 2), f32),
+            pltpu.VMEM((GROUP, 2, 64, quarter // 2), f32),
+            pltpu.VMEM((1, 64, elements), f32),
+            pltpu.VMEM((64, 64), f32),
+            pltpu.VMEM((64, 96), f32),
+            pltpu.VMEM((64, 64), f32),
+            pltpu.VMEM((6, elements), i32),
+            pltpu.VMEM((6, elements), i32),
+            pltpu.VMEM((1, bound), i32),
+            pltpu.VMEM((1, bound), i32),
+            dma((8,)),
+            dma((tiles,)),
             dma((STEPS, 2)),
             dma((STEPS, 2)),
-            dma((GROUP - 1,)),
-            dma((GROUP - 1,)),
-            dma,
-            dma,
-            dma((GROUP - 1,)),
-            dma((GROUP - 1,)),
+            dma((GROUP - 1, 2)),
+            dma((GROUP - 1, 2)),
+            dma((2,)),
+            dma((2,)),
+            dma((GROUP - 1, 2)),
+            dma((GROUP - 1, 2)),
         ],
         compiler_params=pltpu.CompilerParams(
             collective_id=0, has_side_effects=True, vmem_limit_bytes=40 * 1024 * 1024

time: 44.8 us -> 42.6 us (0.951)
  Pallas kernels: 37.4 us -> 35.3 us
    pallas_call x1, Pallas kernels: 37.4 us -> 35.3 us  [shards(): pl.pallas_call(functools.partial(kernel, lax.axis_size('tm'), lax.axis_si...]
where the time goes in v2:
time: 42.6 us; the launch traced here: 42.1 us
  Pallas kernels  35.3 us (83%)
  local copies, waits for them, and re-layouts  6.8 us (16%)
    pallas_call x1, Pallas kernels, shards(): pl.pallas_call(functools.partial(kernel, lax.axis_size('tm'), lax.axis_si...  35.3 us
    unnamed x17, local copies, waits for them, and re-layouts  6.8 us

profile of v2, /device:TPU:25, one launch (start us, length us, event | category | flops | bytes accessed | tf_op | source)
XLA Modules:
  0.0 42.1 jit_solution(1653461211268845870)
XLA Ops:
  0.0 0.0 copy-start.6
  0.0 0.7 %copy-done.6 = s32[512]{0:T(512)S(1)} copy-done((s32[512]{0:T(512)S(1)}, s32[512]{0:T(512)}, u32[]{:S(2)}) %copy-start.6) | copy-done | bytes 2072
  0.7 0.0 copy-start
  0.7 0.9 %copy-done = f32[1,64,1024]{2,1,0:T(8,128)S(1)} copy-done((f32[1,64,1024]{2,1,0:T(8,128)S(1)}, f32[1,64,1024]{2,1,0:T(8,128)}, u32[]{:S(2)}) %copy-start) | copy-done | bytes 262168
  1.6 0.0 copy-start.1
  1.6 0.8 %copy-done.1 = f32[64,64]{1,0:T(8,128)S(1)} copy-done((f32[64,64]{1,0:T(8,128)S(1)}, f32[64,64]{1,0:T(8,128)}, u32[]{:S(2)}) %copy-start.1) | copy-done | bytes 16408
  2.4 0.0 copy-start.2
  2.4 0.8 %copy-done.2 = f32[64,96]{1,0:T(8,128)S(1)} copy-done((f32[64,96]{1,0:T(8,128)S(1)}, f32[64,96]{1,0:T(8,128)}, u32[]{:S(2)}) %copy-start.2) | copy-done | bytes 24600
  3.1 0.0 copy-start.3
  3.2 0.8 %copy-done.3 = f32[64,64]{1,0:T(8,128)S(1)} copy-done((f32[64,64]{1,0:T(8,128)S(1)}, f32[64,64]{1,0:T(8,128)}, u32[]{:S(2)}) %copy-start.3) | copy-done | bytes 16408
  3.9 0.0 copy-start.4
  3.9 0.8 %copy-done.4 = s32[6,1024]{1,0:T(8,128)S(1)} copy-done((s32[6,1024]{1,0:T(8,128)S(1)}, s32[6,1024]{1,0:T(8,128)}, u32[]{:S(2)}) %copy-start.4) | copy-done | bytes 24600
  4.7 0.0 copy-start.5
  4.7 0.8 %copy-done.5 = s32[6,1024]{1,0:T(8,128)S(1)} copy-done((s32[6,1024]{1,0:T(8,128)S(1)}, s32[6,1024]{1,0:T(8,128)}, u32[]{:S(2)}) %copy-start.5) | copy-done | bytes 24600
  5.4 0.0 copy-start.7
  5.4 0.7 %copy-done.7 = s32[512]{0:T(512)S(1)} copy-done((s32[512]{0:T(512)S(1)}, s32[512]{0:T(512)}, u32[]{:S(2)}) %copy-start.7) | copy-done | bytes 2072
  6.1 35.3 %shard_map.82 = f32[1,64,1024]{2,1,0:T(8,128)S(1)} custom-call(f32[1,64,1024]{2,1,0:T(8,128)S(1)} %copy-done, f32[64,64]{1,0:T(8,128)S(1)} %copy-done.1, f32[64,96]{1,0:T(8,128)S(1)} %copy-done.2, f32[64,64]{1,0:T(8,128)S(1)} %copy-done.3, s32[6,1024]{1,0:T(8,128)S(1)} %copy-done.4, s32[6,1024]{1,0:T(8,128)S(1)} %copy-done.5, s32[1,512]{1,0:T(1,128)S(1)} %bitcast.2, ...), custom_call_target="tpu_custom_call" | custom-call | tf_op jit(solution)/shard_map/pallas_call | solution.py:405
  41.4 0.7 %copy.10 = f32[1,64,1024]{2,1,0:T(8,128)} copy(f32[1,64,1024]{2,1,0:T(8,128)S(1)} %shard_map.82) | data formatting | bytes 524288
Async XLA Ops:
  0.0 0.7 %copy-start.6 = (s32[512]{0:T(512)S(1)}, s32[512]{0:T(512)}, u32[]{:S(2)}) copy-start(s32[512]{0:T(512)} %param.14) | copy-start | bytes 6148
  0.7 0.9 %copy-start = (f32[1,64,1024]{2,1,0:T(8,128)S(1)}, f32[1,64,1024]{2,1,0:T(8,128)}, u32[]{:S(2)}) copy-start(f32[1,64,1024]{2,1,0:T(8,128)} %start_ref.1) | copy-start | bytes 786436
  1.6 0.8 %copy-start.1 = (f32[64,64]{1,0:T(8,128)S(1)}, f32[64,64]{1,0:T(8,128)}, u32[]{:S(2)}) copy-start(f32[64,64]{1,0:T(8,128)} %stiff_ref.1) | copy-start | bytes 49156
  2.4 0.8 %copy-start.2 = (f32[64,96]{1,0:T(8,128)S(1)}, f32[64,96]{1,0:T(8,128)}, u32[]{:S(2)}) copy-start(f32[64,96]{1,0:T(8,128)} %lift_ref.1) | copy-start | bytes 73732
  3.1 0.8 %copy-start.3 = (f32[64,64]{1,0:T(8,128)S(1)}, f32[64,64]{1,0:T(8,128)}, u32[]{:S(2)}) copy-start(f32[64,64]{1,0:T(8,128)} %coarse_ref.1) | copy-start | bytes 49156
  3.9 0.8 %copy-start.4 = (s32[6,1024]{1,0:T(8,128)S(1)}, s32[6,1024]{1,0:T(8,128)}, u32[]{:S(2)}) copy-start(s32[6,1024]{1,0:T(8,128)} %near_ref.1) | copy-start | bytes 73732
  4.7 0.8 %copy-start.5 = (s32[6,1024]{1,0:T(8,128)S(1)}, s32[6,1024]{1,0:T(8,128)}, u32[]{:S(2)}) copy-start(s32[6,1024]{1,0:T(8,128)} %turn_ref.1) | copy-start | bytes 73732
  5.4 0.7 %copy-start.7 = (s32[512]{0:T(512)S(1)}, s32[512]{0:T(512)}, u32[]{:S(2)}) copy-start(s32[512]{0:T(512)} %param.15) | copy-start | bytes 6148

commit v3 on v2

--- a/solution.py
+++ b/solution.py
@@ -45,10 +45,9 @@
     return jnp.take_along_axis(value, index, axis=axis, mode="promise_in_bounds")
 
 
-def pick(sources, index):
+def pick(sources, index, upper=None, lower=None):
     lane = index & (LANES - 1)
     tile = index >> 7
-    upper = lower = None
     for number, load in sources:
         first, second = load()
         first, second = along(first, lane, 1), along(second, lane, 1)
@@ -74,7 +73,7 @@
     n_time, n_space,
     start_ref, stiff_ref, lift_ref, coarse_ref, near_ref, turn_ref, low_ref, high_ref,
     out_ref,
-    stack, trace, spot, coarse_start, leave, halo, joined, weights, reach, powers, last_power, one_power,
+    stack, trace, heads, chosen, met, spot, coarse_start, leave, halo, joined, weights, reach, powers, last_power, one_power,
     defect, gathered, carry, ends, final,
     start_in, stiff_in, lift_in, coarse_in, near_in, turn_in, low_in, high_in, load_sem, state_sem,
     halo_send, halo_recv, mix_send, mix_recv, chain_send, chain_recv, back_send, back_recv,
@@ -133,6 +132,14 @@
             trace[tile, 1, 4 * i : 4 * i + 4, :] = stack[tile, 16 * i + 12 : 16 * i + 16, :]
         trace[tile, 2] = stack[tile, pl.ds(0, 16, stride=4), :]
         trace[tile, 3] = stack[tile, pl.ds(3, 16, stride=4), :]
+        for face in range(6):
+            if face < 2:
+                value = stack[tile, 48 * face : 48 * face + 16, :]
+            else:
+                value = trace[tile, face - 2]
+            head, tail = parts_of(value)
+            heads[face, 0:16, tile * LANES : (tile + 1) * LANES] = head
+            heads[face, 16:32, tile * LANES : (tile + 1) * LANES] = tail
 
     loads["low"].wait()
     loads["high"].wait()
@@ -188,17 +195,34 @@
             at = 64 + 16 * face + 8 * half
             stack[t, at : at + 8, :] = turned
 
-    def inner_faces(t, _):
-        for face in range(2, 6):
-            sources = [local_source(face ^ 1, s) for s in range(tiles)]
-            place(face, t, *pick(sources, wide_index(near_in, face, t)))
+    def choose(k, _):
+        row = lax.broadcasted_iota(jnp.int32, (LANES, WIDE), 0) + k * LANES
+        at = pl.multiple_of(k * LANES, LANES)
+        for face in range(6):
+            for c in range(elements // WIDE):
+                index = near_in[face : face + 1, c * WIDE : (c + 1) * WIDE]
+                hit = jnp.where(row == index, 1.0, 0.0).astype(jnp.bfloat16)
+                chosen[face, c, pl.ds(at, LANES), :] = hit
+        return 0
+
+    def local_faces(c, _):
+        for face in (2, 3, 4, 5, 0, 1):
+            both = jnp.dot(heads[face ^ 1], chosen[face, c], preferred_element_type=jnp.float32)
+            value = both[0:16] + both[16:32]
+            for piece in range(WIDE // LANES):
+                t = c * (WIDE // LANES) + piece
+                part = value[:, piece * LANES : (piece + 1) * LANES]
+                if face < 2:
+                    met[face, t] = part
+                else:
+                    place(face, t, part[0:8], part[8:16])
         return 0
 
     def outer_faces(step):
         def body(t, _):
             for face in range(2):
                 side = 1 - face
-                sources = [local_source(face ^ 1, s) for s in range(tiles)]
+                sources = []
                 for b in range(bound_tiles):
                     number = tiles + face * bound_tiles + b
                     sources.append(
@@ -210,7 +234,8 @@
                             ),
                         )
                     )
-                place(face, t, *pick(sources, wide_index(near_in, face, t)))
+                inside = met[face, t, 0:8, :], met[face, t, 8:16, :]
+                place(face, t, *pick(sources, wide_index(near_in, face, t), *inside))
             return 0
 
         return body
@@ -284,7 +309,8 @@
         if step == 0:
             fine_matrix()
             loads["near"].wait()
-        lax.fori_loop(0, tiles, inner_faces, 0, unroll=4)
+            lax.fori_loop(0, tiles, choose, 0)
+        lax.fori_loop(0, elements // WIDE, local_faces, 0, unroll=2)
         if step == 1:
             coarse_matrices()
         if step == 2:
@@ -410,6 +436,9 @@
         scratch_shapes=[
             pltpu.VMEM((tiles, 160, LANES), f32),
             pltpu.VMEM((tiles, 4, 16, LANES), f32),
+            pltpu.VMEM((6, 32, elements), b16),
+            pltpu.VMEM((6, elements // WIDE, elements, WIDE), b16),
+            pltpu.VMEM((2, tiles, 16, LANES), f32),
             pltpu.VMEM((6, tiles, 16, LANES), i32),
             pltpu.VMEM((elements // WIDE, 64, WIDE), f32),
             pltpu.VMEM((STEPS, 2, bound_tiles, 16, LANES), f32),
@@ -445,7 +474,7 @@
             dma((GROUP - 1, 2)),
         ],
         compiler_params=pltpu.CompilerParams(
-            collective_id=0, has_side_effects=True, vmem_limit_bytes=40 * 1024 * 1024
+            collective_id=0, has_side_effects=True, vmem_limit_bytes=63 * 1024 * 1024
         ),
     )(
         start_state, stiffness, lifting, coarse, neighbor, orientation,

time: 42.6 us -> 35.3 us (0.83)
  local copies, waits for them, and re-layouts: 6.8 us -> 1.67 us
  Pallas kernels: 35.3 us -> 33.4 us
    unnamed x17 -> x1, local copies, waits for them, and re-layouts: 6.8 us -> 1.67 us
    pallas_call x1, Pallas kernels: 35.3 us -> 33.4 us  [shards(): pl.pallas_call(functools.partial(kernel, lax.axis_size('tm'), lax.axis_si...]
where the time goes in v3:
time: 35.3 us; the launch traced here: 35.1 us
  Pallas kernels  33.4 us (95%)
  local copies, waits for them, and re-layouts  1.67 us (5%)
    pallas_call x1, Pallas kernels, shards(): pl.pallas_call(functools.partial(kernel, lax.axis_size('tm'), lax.axis_si...  33.4 us
    unnamed x1, local copies, waits for them, and re-layouts  1.67 us

profile of v3, /device:TPU:25, one launch (start us, length us, event | category | flops | bytes accessed | tf_op | source)
XLA Modules:
  0.0 35.1 jit_solution(11659991697775812165)
XLA Ops:
  0.0 33.4 %shard_map.82 = f32[1,64,1024]{2,1,0:T(8,128)} custom-call(f32[1,64,1024]{2,1,0:T(8,128)} %start_ref.1, f32[64,64]{1,0:T(8,128)} %stiff_ref.1, f32[64,96]{1,0:T(8,128)} %lift_ref.1, f32[64,64]{1,0:T(8,128)} %coarse_ref.1, s32[6,1024]{1,0:T(8,128)} %near_ref.1, s32[6,1024]{1,0:T(8,128)} %turn_ref.1, s32[1,512]{1,0:T(1,128)} %bitcast.2, s32[1,512]{1,0:T(1,128)} %bitcast.3), custom_call_target="tpu_custom_call" | custom-call | tf_op jit(solution)/shard_map/pallas_call | solution.py:431
  33.5 1.7 %copy.10 = f32[1,64,1024]{2,1,0:T(8,128)} copy(f32[1,64,1024]{2,1,0:T(8,128)} %shard_map.82) | data formatting | bytes 524288

commit v4 on v3

--- a/solution.py
+++ b/solution.py
@@ -73,7 +73,7 @@
     n_time, n_space,
     start_ref, stiff_ref, lift_ref, coarse_ref, near_ref, turn_ref, low_ref, high_ref,
     out_ref,
-    stack, trace, heads, chosen, met, spot, coarse_start, leave, halo, joined, weights, reach, powers, last_power, one_power,
+    stack, trace, heads, chosen, send_hot, meet_hot, met, spot, coarse_start, leave, halo, joined, weights, reach, powers, last_power, one_power,
     defect, gathered, carry, ends, final,
     start_in, stiff_in, lift_in, coarse_in, near_in, turn_in, low_in, high_in, load_sem, state_sem,
     halo_send, halo_recv, mix_send, mix_recv, chain_send, chain_recv, back_send, back_recv,
@@ -107,6 +107,7 @@
         states[-1].start()
     for name in ("turn", "stiff", "lift", "near", "coarse", "start"):
         loads[name].start()
+    small = elements <= 1024
     tiles = elements // LANES
     bound = low_ref.shape[1]
     bound_tiles = bound // LANES
@@ -126,20 +127,23 @@
     for time in mates + [following, previous]:
         pl.semaphore_signal(barrier, inc=1, device_id=(time, me_s), device_id_type=MESH)
 
-    def keep_traces(tile):
+    def keep_parts(face, tile, value):
+        head, tail = parts_of(value)
+        heads[face, 0:16, tile * LANES : (tile + 1) * LANES] = head
+        heads[face, 16:32, tile * LANES : (tile + 1) * LANES] = tail
+
+    def keep_outer(tile):
+        for face in range(2):
+            keep_parts(face, tile, stack[tile, 48 * face : 48 * face + 16, :])
+
+    def keep_inner(tile):
         for i in range(4):
             trace[tile, 0, 4 * i : 4 * i + 4, :] = stack[tile, 16 * i : 16 * i + 4, :]
             trace[tile, 1, 4 * i : 4 * i + 4, :] = stack[tile, 16 * i + 12 : 16 * i + 16, :]
         trace[tile, 2] = stack[tile, pl.ds(0, 16, stride=4), :]
         trace[tile, 3] = stack[tile, pl.ds(3, 16, stride=4), :]
-        for face in range(6):
-            if face < 2:
-                value = stack[tile, 48 * face : 48 * face + 16, :]
-            else:
-                value = trace[tile, face - 2]
-            head, tail = parts_of(value)
-            heads[face, 0:16, tile * LANES : (tile + 1) * LANES] = head
-            heads[face, 16:32, tile * LANES : (tile + 1) * LANES] = tail
+        for face in range(2, 6):
+            keep_parts(face, tile, trace[tile, face - 2])
 
     loads["low"].wait()
     loads["high"].wait()
@@ -179,7 +183,14 @@
                 leave[step, side, t, 8:16, :] = lower
             return 0
 
-        lax.fori_loop(0, bound_tiles, fill, 0, unroll=4)
+        if step == 0 or not small:
+            lax.fori_loop(0, bound_tiles, fill, 0, unroll=4)
+        else:
+            for side in range(2):
+                both = jnp.dot(heads[side], send_hot[side], preferred_element_type=jnp.float32)
+                value = both[0:16] + both[16:32]
+                for b in range(bound_tiles):
+                    leave[step, side, b] = value[:, b * LANES : (b + 1) * LANES]
         if step == 0:
             pl.semaphore_wait(barrier, 2 + GROUP - 1 + 2)
         copies = halo_copies(step)
@@ -195,15 +206,48 @@
             at = 64 + 16 * face + 8 * half
             stack[t, at : at + 8, :] = turned
 
+    def one_hot(index, k):
+        row = lax.broadcasted_iota(jnp.int32, (LANES, index.shape[1]), 0)
+        row = row.astype(jnp.float32).astype(jnp.bfloat16)
+        inside = jnp.clip(index - k * LANES, -1, LANES).astype(jnp.float32).astype(jnp.bfloat16)
+        inside = jnp.broadcast_to(inside, row.shape)
+        return jnp.where(row == inside, jnp.ones_like(row), jnp.zeros_like(row))
+
     def choose(k, _):
-        row = lax.broadcasted_iota(jnp.int32, (LANES, WIDE), 0) + k * LANES
-        at = pl.multiple_of(k * LANES, LANES)
+        at = pl.ds(pl.multiple_of(k * LANES, LANES), LANES)
         for face in range(6):
             for c in range(elements // WIDE):
                 index = near_in[face : face + 1, c * WIDE : (c + 1) * WIDE]
-                hit = jnp.where(row == index, 1.0, 0.0).astype(jnp.bfloat16)
-                chosen[face, c, pl.ds(at, LANES), :] = hit
+                chosen[face, c, at, :] = one_hot(index, k)
         return 0
+
+    def choose_sent(k, _):
+        at = pl.ds(pl.multiple_of(k * LANES, LANES), LANES)
+        for side, ref in ((0, low_in), (1, high_in)):
+            send_hot[side, at, :] = one_hot(ref[...], k)
+        return 0
+
+    def choose_met(k, _):
+        at = pl.ds(pl.multiple_of(k * LANES, LANES), LANES)
+        for face in range(2):
+            for c in range(elements // WIDE):
+                index = near_in[face : face + 1, c * WIDE : (c + 1) * WIDE]
+                meet_hot[face, c, at, :] = one_hot(index - (elements + face * bound), k)
+        return 0
+
+    def halo_parts(step, face):
+        tiles_in = [halo[step, 1 - face, b] for b in range(bound_tiles)]
+        head, tail = parts_of(jnp.concatenate(tiles_in, axis=1))
+        return jnp.concatenate([head, tail], axis=0)
+
+    def meet(c, parts):
+        for face in range(2):
+            both = jnp.dot(parts[face], meet_hot[face, c], preferred_element_type=jnp.float32)
+            value = both[0:16] + both[16:32]
+            for piece in range(WIDE // LANES):
+                t = c * (WIDE // LANES) + piece
+                part = met[face, t] + value[:, piece * LANES : (piece + 1) * LANES]
+                place(face, t, part[0:8], part[8:16])
 
     def local_faces(c, _):
         for face in (2, 3, 4, 5, 0, 1):
@@ -256,7 +300,8 @@
     loads["turn"].wait()
     lax.fori_loop(0, tiles, spots, 0)
     for tile in range(tiles):
-        keep_traces(tile)
+        keep_outer(tile)
+        keep_inner(tile)
 
     def fine_matrix():
         loads["stiff"].wait()
@@ -303,13 +348,18 @@
 
     for step in range(STEPS):
         if step > 0:
+            for tile in range(tiles):
+                keep_outer(tile)
             copies = send_halo(step)
             for tile in range(tiles):
-                keep_traces(tile)
+                keep_inner(tile)
         if step == 0:
             fine_matrix()
             loads["near"].wait()
             lax.fori_loop(0, tiles, choose, 0)
+            if small:
+                lax.fori_loop(0, bound_tiles, choose_met, 0)
+                lax.fori_loop(0, tiles, choose_sent, 0)
         lax.fori_loop(0, elements // WIDE, local_faces, 0, unroll=2)
         if step == 1:
             coarse_matrices()
@@ -317,7 +367,12 @@
             coarse_first()
         for copy in copies:
             copy.wait()
-        lax.fori_loop(0, tiles, outer_faces(step), 0, unroll=4)
+        if small:
+            parts = [halo_parts(step, face) for face in range(2)]
+            for c in range(elements // WIDE):
+                meet(c, parts)
+        else:
+            lax.fori_loop(0, tiles, outer_faces(step), 0, unroll=4)
         if step < STEPS - 1:
             for c in range(elements // WIDE):
                 later = advance(c)
@@ -438,6 +493,8 @@
             pltpu.VMEM((tiles, 4, 16, LANES), f32),
             pltpu.VMEM((6, 32, elements), b16),
             pltpu.VMEM((6, elements // WIDE, elements, WIDE), b16),
+            pltpu.VMEM((2, elements, bound) if elements <= 1024 else (1, 16, LANES), b16),
+            pltpu.VMEM((2, elements // WIDE, bound, WIDE) if elements <= 1024 else (1, 1, 16, LANES), b16),
             pltpu.VMEM((2, tiles, 16, LANES), f32),
             pltpu.VMEM((6, tiles, 16, LANES), i32),
             pltpu.VMEM((elements // WIDE, 64, WIDE), f32),

time: 35.3 us -> 35.7 us (1.011)
  Pallas kernels: 33.4 us -> 33.9 us
    pallas_call x1, Pallas kernels: 33.4 us -> 33.9 us  [shards(): pl.pallas_call(functools.partial(kernel, lax.axis_size('tm'), lax.axis_si...]
where the time goes in v4:
time: 35.7 us; the launch traced here: 35.6 us
  Pallas kernels  33.9 us (95%)
  local copies, waits for them, and re-layouts  1.67 us (5%)
    pallas_call x1, Pallas kernels, shards(): pl.pallas_call(functools.partial(kernel, lax.axis_size('tm'), lax.axis_si...  33.9 us
    unnamed x1, local copies, waits for them, and re-layouts  1.67 us

profile of v4, /device:TPU:25, one launch (start us, length us, event | category | flops | bytes accessed | tf_op | source)
XLA Modules:
  0.0 35.6 jit_solution(13736598837743397312)
XLA Ops:
  0.0 33.9 %shard_map.82 = f32[1,64,1024]{2,1,0:T(8,128)} custom-call(f32[1,64,1024]{2,1,0:T(8,128)} %start_ref.1, f32[64,64]{1,0:T(8,128)} %stiff_ref.1, f32[64,96]{1,0:T(8,128)} %lift_ref.1, f32[64,64]{1,0:T(8,128)} %coarse_ref.1, s32[6,1024]{1,0:T(8,128)} %near_ref.1, s32[6,1024]{1,0:T(8,128)} %turn_ref.1, s32[1,512]{1,0:T(1,128)} %bitcast.2, s32[1,512]{1,0:T(1,128)} %bitcast.3), custom_call_target="tpu_custom_call" | custom-call | tf_op jit(solution)/shard_map/pallas_call | solution.py:486
  33.9 1.7 %copy.10 = f32[1,64,1024]{2,1,0:T(8,128)} copy(f32[1,64,1024]{2,1,0:T(8,128)} %shard_map.82) | data formatting | bytes 524288

commit v5 on v4

--- a/solution.py
+++ b/solution.py
@@ -108,6 +108,7 @@
     for name in ("turn", "stiff", "lift", "near", "coarse", "start"):
         loads[name].start()
     small = elements <= 1024
+    by_product, by_gather = (1, 3, 4, 5), (0, 2)
     tiles = elements // LANES
     bound = low_ref.shape[1]
     bound_tiles = bound // LANES
@@ -175,22 +176,22 @@
         ]
 
     def send_halo(step):
-        def fill(t, _):
-            for side, ref in ((0, low_in), (1, high_in)):
-                sources = [local_source(side, s) for s in range(tiles)]
-                upper, lower = pick(sources, wide_index(ref, 0, t))
-                leave[step, side, t, 0:8, :] = upper
-                leave[step, side, t, 8:16, :] = lower
-            return 0
-
-        if step == 0 or not small:
-            lax.fori_loop(0, bound_tiles, fill, 0, unroll=4)
-        else:
-            for side in range(2):
-                both = jnp.dot(heads[side], send_hot[side], preferred_element_type=jnp.float32)
-                value = both[0:16] + both[16:32]
-                for b in range(bound_tiles):
-                    leave[step, side, b] = value[:, b * LANES : (b + 1) * LANES]
+        def fill(side, ref, t):
+            sources = [local_source(side, s) for s in range(tiles)]
+            upper, lower = pick(sources, wide_index(ref, 0, t))
+            leave[step, side, t, 0:8, :] = upper
+            leave[step, side, t, 8:16, :] = lower
+
+        both_sides = step == 0 or not small
+        if not both_sides:
+            both = jnp.dot(heads[1], send_hot[...], preferred_element_type=jnp.float32)
+            value = both[0:16] + both[16:32]
+            for b in range(bound_tiles):
+                leave[step, 1, b] = value[:, b * LANES : (b + 1) * LANES]
+        for t in range(bound_tiles):
+            fill(0, low_in, t)
+            if both_sides:
+                fill(1, high_in, t)
         if step == 0:
             pl.semaphore_wait(barrier, 2 + GROUP - 1 + 2)
         copies = halo_copies(step)
@@ -215,24 +216,22 @@
 
     def choose(k, _):
         at = pl.ds(pl.multiple_of(k * LANES, LANES), LANES)
-        for face in range(6):
+        for number, face in enumerate(by_product):
             for c in range(elements // WIDE):
                 index = near_in[face : face + 1, c * WIDE : (c + 1) * WIDE]
-                chosen[face, c, at, :] = one_hot(index, k)
+                chosen[number, c, at, :] = one_hot(index, k)
         return 0
 
     def choose_sent(k, _):
         at = pl.ds(pl.multiple_of(k * LANES, LANES), LANES)
-        for side, ref in ((0, low_in), (1, high_in)):
-            send_hot[side, at, :] = one_hot(ref[...], k)
+        send_hot[at, :] = one_hot(high_in[...], k)
         return 0
 
     def choose_met(k, _):
         at = pl.ds(pl.multiple_of(k * LANES, LANES), LANES)
-        for face in range(2):
-            for c in range(elements // WIDE):
-                index = near_in[face : face + 1, c * WIDE : (c + 1) * WIDE]
-                meet_hot[face, c, at, :] = one_hot(index - (elements + face * bound), k)
+        for c in range(elements // WIDE):
+            index = near_in[1:2, c * WIDE : (c + 1) * WIDE]
+            meet_hot[c, at, :] = one_hot(index - (elements + bound), k)
         return 0
 
     def halo_parts(step, face):
@@ -240,18 +239,38 @@
         head, tail = parts_of(jnp.concatenate(tiles_in, axis=1))
         return jnp.concatenate([head, tail], axis=0)
 
-    def meet(c, parts):
-        for face in range(2):
-            both = jnp.dot(parts[face], meet_hot[face, c], preferred_element_type=jnp.float32)
-            value = both[0:16] + both[16:32]
-            for piece in range(WIDE // LANES):
-                t = c * (WIDE // LANES) + piece
-                part = met[face, t] + value[:, piece * LANES : (piece + 1) * LANES]
-                place(face, t, part[0:8], part[8:16])
+    def halo_sources(step, face):
+        sources = []
+        for b in range(bound_tiles):
+            number = tiles + face * bound_tiles + b
+            sources.append(
+                (
+                    number,
+                    lambda b=b: (
+                        halo[step, 1 - face, b, 0:8, :],
+                        halo[step, 1 - face, b, 8:16, :],
+                    ),
+                )
+            )
+        return sources
+
+    def meet_gather(step, face, t):
+        inside = met[face, t, 0:8, :], met[face, t, 8:16, :]
+        index = wide_index(near_in, face, t)
+        place(face, t, *pick(halo_sources(step, face), index, *inside))
+
+    def meet(step, c, parts):
+        both = jnp.dot(parts, meet_hot[c], preferred_element_type=jnp.float32)
+        value = both[0:16] + both[16:32]
+        for piece in range(WIDE // LANES):
+            t = c * (WIDE // LANES) + piece
+            part = met[1, t] + value[:, piece * LANES : (piece + 1) * LANES]
+            place(1, t, part[0:8], part[8:16])
+            meet_gather(step, 0, t)
 
     def local_faces(c, _):
-        for face in (2, 3, 4, 5, 0, 1):
-            both = jnp.dot(heads[face ^ 1], chosen[face, c], preferred_element_type=jnp.float32)
+        for number, face in enumerate(by_product):
+            both = jnp.dot(heads[face ^ 1], chosen[number, c], preferred_element_type=jnp.float32)
             value = both[0:16] + both[16:32]
             for piece in range(WIDE // LANES):
                 t = c * (WIDE // LANES) + piece
@@ -260,26 +279,22 @@
                     met[face, t] = part
                 else:
                     place(face, t, part[0:8], part[8:16])
+        for face in by_gather:
+            sources = [local_source(face ^ 1, s) for s in range(tiles)]
+            for piece in range(WIDE // LANES):
+                t = c * (WIDE // LANES) + piece
+                upper, lower = pick(sources, wide_index(near_in, face, t))
+                if face < 2:
+                    met[face, t, 0:8, :] = upper
+                    met[face, t, 8:16, :] = lower
+                else:
+                    place(face, t, upper, lower)
         return 0
 
     def outer_faces(step):
         def body(t, _):
             for face in range(2):
-                side = 1 - face
-                sources = []
-                for b in range(bound_tiles):
-                    number = tiles + face * bound_tiles + b
-                    sources.append(
-                        (
-                            number,
-                            lambda b=b: (
-                                halo[step, side, b, 0:8, :],
-                                halo[step, side, b, 8:16, :],
-                            ),
-                        )
-                    )
-                inside = met[face, t, 0:8, :], met[face, t, 8:16, :]
-                place(face, t, *pick(sources, wide_index(near_in, face, t), *inside))
+                meet_gather(step, face, t)
             return 0
 
         return body
@@ -360,7 +375,7 @@
             if small:
                 lax.fori_loop(0, bound_tiles, choose_met, 0)
                 lax.fori_loop(0, tiles, choose_sent, 0)
-        lax.fori_loop(0, elements // WIDE, local_faces, 0, unroll=2)
+        lax.fori_loop(0, elements // WIDE, local_faces, 0, unroll=4)
         if step == 1:
             coarse_matrices()
         if step == 2:
@@ -368,9 +383,9 @@
         for copy in copies:
             copy.wait()
         if small:
-            parts = [halo_parts(step, face) for face in range(2)]
+            parts = halo_parts(step, 1)
             for c in range(elements // WIDE):
-                meet(c, parts)
+                meet(step, c, parts)
         else:
             lax.fori_loop(0, tiles, outer_faces(step), 0, unroll=4)
         if step < STEPS - 1:
@@ -492,9 +507,9 @@
             pltpu.VMEM((tiles, 160, LANES), f32),
             pltpu.VMEM((tiles, 4, 16, LANES), f32),
             pltpu.VMEM((6, 32, elements), b16),
-            pltpu.VMEM((6, elements // WIDE, elements, WIDE), b16),
-            pltpu.VMEM((2, elements, bound) if elements <= 1024 else (1, 16, LANES), b16),
-            pltpu.VMEM((2, elements // WIDE, bound, WIDE) if elements <= 1024 else (1, 1, 16, LANES), b16),
+            pltpu.VMEM((4, elements // WIDE, elements, WIDE), b16),
+            pltpu.VMEM((elements, bound) if elements <= 1024 else (16, LANES), b16),
+            pltpu.VMEM((elements // WIDE, bound, WIDE) if elements <= 1024 else (1, 16, LANES), b16),
             pltpu.VMEM((2, tiles, 16, LANES), f32),
             pltpu.VMEM((6, tiles, 16, LANES), i32),
             pltpu.VMEM((elements // WIDE, 64, WIDE), f32),

time: 35.7 us -> 33.9 us (0.950)
  Pallas kernels: 33.9 us -> 32.1 us
    pallas_call x1, Pallas kernels: 33.9 us -> 32.1 us  [shards(): pl.pallas_call(functools.partial(kernel, lax.axis_size('tm'), lax.axis_si...]
where the time goes in v5:
time: 33.9 us; the launch traced here: 33.8 us
  Pallas kernels  32.1 us (95%)
  local copies, waits for them, and re-layouts  1.67 us (5%)
    pallas_call x1, Pallas kernels, shards(): pl.pallas_call(functools.partial(kernel, lax.axis_size('tm'), lax.axis_si...  32.1 us
    unnamed x1, local copies, waits for them, and re-layouts  1.67 us

profile of v5, /device:TPU:25, one launch (start us, length us, event | category | flops | bytes accessed | tf_op | source)
XLA Modules:
  0.0 33.8 jit_solution(1547917295939697864)
XLA Ops:
  0.0 32.1 %shard_map.82 = f32[1,64,1024]{2,1,0:T(8,128)} custom-call(f32[1,64,1024]{2,1,0:T(8,128)} %start_ref.1, f32[64,64]{1,0:T(8,128)} %stiff_ref.1, f32[64,96]{1,0:T(8,128)} %lift_ref.1, f32[64,64]{1,0:T(8,128)} %coarse_ref.1, s32[6,1024]{1,0:T(8,128)} %near_ref.1, s32[6,1024]{1,0:T(8,128)} %turn_ref.1, s32[1,512]{1,0:T(1,128)} %bitcast.2, s32[1,512]{1,0:T(1,128)} %bitcast.3), custom_call_target="tpu_custom_call" | custom-call | tf_op jit(solution)/shard_map/pallas_call | solution.py:501
  32.1 1.7 %copy.10 = f32[1,64,1024]{2,1,0:T(8,128)} copy(f32[1,64,1024]{2,1,0:T(8,128)} %shard_map.82) | data formatting | bytes 524288

commit v6 on v5

--- a/solution.py
+++ b/solution.py
@@ -73,7 +73,7 @@
     n_time, n_space,
     start_ref, stiff_ref, lift_ref, coarse_ref, near_ref, turn_ref, low_ref, high_ref,
     out_ref,
-    stack, trace, heads, chosen, send_hot, meet_hot, met, spot, coarse_start, leave, halo, joined, weights, reach, powers, last_power, one_power,
+    stack, trace, heads, chosen, send_hot, meet_hot, met, spot, coarse_start, leave, halo, joined, weights, outer_weights, base, reach, powers, last_power, one_power,
     defect, gathered, carry, ends, final,
     start_in, stiff_in, lift_in, coarse_in, near_in, turn_in, low_in, high_in, load_sem, state_sem,
     halo_send, halo_recv, mix_send, mix_recv, chain_send, chain_recv, back_send, back_recv,
@@ -327,15 +327,15 @@
         unit = jnp.where(row64 == col64, 1.0, 0.0).astype(jnp.float32)
         joined[:, 0:64] = stiff_in[...] - exact(lifting, selection()) + unit
         joined[:, 64:160] = lifting
-        keep_split(weights, joined[...])
+        whole = joined[...]
+        keep_split(weights, jnp.concatenate([whole[:, 0:64], whole[:, 96:160]], axis=1))
+        keep_split(outer_weights, whole[:, 64:96])
 
     def coarse_matrices():
-        loads["coarse"].wait()
         one = coarse_in[...]
         two = exact(one, one)
         three = exact(two, one)
         four = exact(two, two)
-        keep_split(one_power, one)
         keep_split(last_power, four)
         for part in range(2):
             for at, power in enumerate((one, two, three)):
@@ -351,15 +351,21 @@
 
     def coarse_first():
         loads["start"].wait()
+        loads["coarse"].wait()
+        keep_split(one_power, coarse_in[...])
         for c in range(elements // WIDE):
             columns = start_in[0, :, c * WIDE : (c + 1) * WIDE]
             coarse_start[c] = jnp.where(me_t == 0, 0.0, split_dot(one_power, columns))
 
-    def advance(c):
+    def begin(c):
         operand = jnp.concatenate([stack[2 * c], stack[2 * c + 1]], axis=1)
         state = operand[0:64]
-        rate = split_dot(weights, operand) - state * state * state
-        return state + time_step * rate
+        known = jnp.concatenate([state, operand[96:160]], axis=0)
+        base[c] = state + time_step * (split_dot(weights, known) - state * state * state)
+
+    def advance(c):
+        outer = jnp.concatenate([stack[2 * c, 64:96, :], stack[2 * c + 1, 64:96, :]], axis=1)
+        return base[c] + time_step * split_dot(outer_weights, outer)
 
     for step in range(STEPS):
         if step > 0:
@@ -376,8 +382,8 @@
                 lax.fori_loop(0, bound_tiles, choose_met, 0)
                 lax.fori_loop(0, tiles, choose_sent, 0)
         lax.fori_loop(0, elements // WIDE, local_faces, 0, unroll=4)
-        if step == 1:
-            coarse_matrices()
+        for c in range(elements // WIDE):
+            begin(c)
         if step == 2:
             coarse_first()
         for copy in copies:
@@ -425,6 +431,7 @@
     for by in (2, 3, 1):
         mixes[by, 1].start()
     last_step(rank, gathered, rank)
+    coarse_matrices()
 
     chain = [
         pltpu.make_async_remote_copy(
@@ -516,7 +523,9 @@
             pltpu.VMEM((STEPS, 2, bound_tiles, 16, LANES), f32),
             pltpu.VMEM((STEPS, 2, bound_tiles, 16, LANES), f32),
             pltpu.VMEM((64, 160), f32),
-            pltpu.VMEM((128, 160), b16),
+            pltpu.VMEM((128, 128), b16),
+            pltpu.VMEM((128, 32), b16),
+            pltpu.VMEM((elements // WIDE, 64, WIDE), f32),
             pltpu.VMEM((384, 192), b16),
             pltpu.VMEM((384, 64), b16),
             pltpu.VMEM((128, 64), b16),

time: 33.9 us -> 33.9 us (level)
  no operation moved by 1% of the time
where the time goes in v6:
time: 33.9 us; the launch traced here: 33.7 us
  Pallas kernels  32.1 us (95%)
  local copies, waits for them, and re-layouts  1.67 us (5%)
    pallas_call x1, Pallas kernels, shards(): pl.pallas_call(functools.partial(kernel, lax.axis_size('tm'), lax.axis_si...  32.1 us
    unnamed x1, local copies, waits for them, and re-layouts  1.67 us

profile of v6, /device:TPU:25, one launch (start us, length us, event | category | flops | bytes accessed | tf_op | source)
XLA Modules:
  0.0 33.7 jit_solution(10234627727416277767)
XLA Ops:
  0.0 32.1 %shard_map.82 = f32[1,64,1024]{2,1,0:T(8,128)} custom-call(f32[1,64,1024]{2,1,0:T(8,128)} %start_ref.1, f32[64,64]{1,0:T(8,128)} %stiff_ref.1, f32[64,96]{1,0:T(8,128)} %lift_ref.1, f32[64,64]{1,0:T(8,128)} %coarse_ref.1, s32[6,1024]{1,0:T(8,128)} %near_ref.1, s32[6,1024]{1,0:T(8,128)} %turn_ref.1, s32[1,512]{1,0:T(1,128)} %bitcast.2, s32[1,512]{1,0:T(1,128)} %bitcast.3), custom_call_target="tpu_custom_call" | custom-call | tf_op jit(solution)/shard_map/pallas_call | solution.py:508
  32.1 1.7 %copy.10 = f32[1,64,1024]{2,1,0:T(8,128)} copy(f32[1,64,1024]{2,1,0:T(8,128)} %shard_map.82) | data formatting | bytes 524288
